TPU v7x, 128 devices: a whole 4x4x4 slice. The times are simulated.
128 devices in a mesh: step: 8 (over z, x_hi), tok: 16 (over y, x_lo, core).
Axes of the slice: x: 4 (x_hi: 2, x_lo: 2; x = x_hi * 2 + x_lo), y: 4, z: 4, core: 2. Of those that a mesh axis runs over, the one named last changes fastest.
Arguments:
- latents: bfloat16 [8, 8192, 1152], P('step', 'tok'), may hold values from -6 to 6
- timesteps: int32 [32], replicated, may hold values from 0 to 63
- experts: int32 [32], replicated, may hold values from 0 to 1
- offset: int32 [1], replicated, may hold values from 0 to 24
- modulation: float32 [64, 3, 1152], replicated, may hold values from -4 to 4
- coef: float32 [64], replicated, may hold values from 0.1 to 1
- w_qkv: bfloat16 [2, 1152, 16, 216], P(None, None, 'tok'), may hold values from -1 to 1
- w_o: bfloat16 [2, 1152, 1152], P(None, 'tok'), may hold values from -0.1875 to 0.1875
- w_cq: bfloat16 [2, 1152, 1152], P(None, None, 'tok'), may hold values from -0.1875 to 0.1875
- w_co: bfloat16 [2, 1152, 1152], P(None, 'tok'), may hold values from -0.1875 to 0.1875
- text_kv: bfloat16 [2, 2, 300, 1152], replicated, may hold values from -240 to 240
Outputs:
- new_latents: bfloat16 [8, 8192, 1152], P('step', 'tok')
All inputs are finite; a program needn't handle non-finite values.
Results may differ from a plain program's by a relative error of at most 0.028.
The roundings to bfloat16 on the way count: a program that leaves them out, or rounds other values in their place, can miss the bound.
Values may be sent and summed in bfloat16 or wider, within the bound.
No kernel may reach another device: no remote copies, remote signals or barrier semaphores. Data moves between devices by JAX's collectives and lax.ppermute only.
A program may use at most 128 MiB of HBM per device.

v0:
```python
import jax
import jax.numpy as jnp
from jax import lax
from jax.sharding import PartitionSpec as P


def from_root(block, axis, holder):
    block = jnp.where(lax.axis_index(axis) == holder, block, jnp.zeros_like(block))
    return lax.psum(block, axis)


def carried_in(value, axis, join, neutral):
    place = lax.axis_index(axis)
    gathered = lax.all_gather(value.astype(jnp.bfloat16), axis)
    state = jnp.zeros_like(value) + jnp.asarray(neutral, value.dtype)

    def one(step, state):
        return join(state, lax.dynamic_index_in_dim(gathered, step, 0, False).astype(value.dtype))

    return lax.fori_loop(0, place, one, state)


def attend(queries, keys, values):
    scale = 1.0 / queries.shape[-1] ** 0.5
    scores = jnp.einsum("qhc,khc->hqk", queries, keys, preferred_element_type=jnp.float32) * scale
    scores = scores - jnp.max(scores, axis=-1, keepdims=True)
    expsc = jnp.exp(scores)
    total = jnp.sum(expsc, axis=-1)
    out = jnp.einsum(
        "hqk,khc->qhc", expsc.astype(jnp.bfloat16), values, preferred_element_type=jnp.float32
    )
    return (out / jnp.transpose(total)[:, :, None]).astype(jnp.bfloat16)


def blocked(queries, keys, values):
    count = queries.shape[0]
    block_rows = min(512, count)
    shaped = queries.reshape(count // block_rows, block_rows, queries.shape[1], queries.shape[2])
    result = lax.map(lambda part: attend(part, keys, values), shaped)
    return result.reshape(count, queries.shape[1], queries.shape[2])


def self_attend(qkv):
    head_size = qkv.shape[2] // 3
    return blocked(
        qkv[:, :, :head_size], qkv[:, :, head_size : 2 * head_size], qkv[:, :, 2 * head_size :]
    )


def attend_group(grouped):
    return self_attend(grouped[:, 0])[:, None]


def body(latents, timesteps, experts, offset, modulation, coef, w_qkv, w_o, w_cq, w_co, text_kv):
    step_index = lax.axis_index("step")
    position = offset[0] + step_index
    entry = lax.dynamic_index_in_dim(timesteps, position, 0, False)
    expert = lax.dynamic_index_in_dim(experts, position, 0, False)
    modulate = lax.dynamic_index_in_dim(modulation, entry, 0, False)
    step_coef = lax.dynamic_index_in_dim(coef, entry, 0, False)
    latent = latents[0]
    width = latent.shape[1]
    head_size = w_qkv.shape[3] // 3
    groups = lax.axis_size("tok")
    flat = latent.astype(jnp.float32)
    mean = jnp.mean(flat, axis=1, keepdims=True)
    var = jnp.mean((flat - mean) ** 2, axis=1, keepdims=True)
    normed = ((flat - mean) * lax.rsqrt(var + 1e-06) * (1.0 + modulate[1]) + modulate[0]).astype(
        jnp.bfloat16
    )
    own_qkv = lax.dynamic_index_in_dim(w_qkv, expert, 0, False)
    qkv = jnp.einsum(
        "td,dhc->thc",
        normed,
        lax.all_gather(own_qkv, "tok", axis=1, tiled=True),
        preferred_element_type=jnp.float32,
    ).astype(jnp.bfloat16)
    grouped = qkv.reshape(qkv.shape[0], groups, qkv.shape[1] // groups, qkv.shape[2])
    head_out = attend_group(lax.all_to_all(grouped, "tok", split_axis=1, concat_axis=0, tiled=True))
    returned = lax.all_to_all(head_out, "tok", split_axis=0, concat_axis=1, tiled=True)
    attended = returned.reshape(returned.shape[0], width)

    def fold_rows(left, piece):
        return jnp.dot(left, piece, preferred_element_type=jnp.float32)

    own_out = lax.dynamic_index_in_dim(w_o, expert, 0, False)
    projected = fold_rows(attended, lax.all_gather(own_out, "tok", axis=0, tiled=True))
    hidden = (flat + modulate[2] * projected).astype(jnp.bfloat16)
    own_cq = lax.dynamic_index_in_dim(w_cq, expert, 0, False)
    cross_q = jnp.dot(
        hidden,
        lax.all_gather(own_cq, "tok", axis=1, tiled=True),
        preferred_element_type=jnp.float32,
    ).astype(jnp.bfloat16)
    own_text = lax.dynamic_index_in_dim(text_kv, expert, 0, False)
    heads = width // head_size
    text_keys = own_text[0].reshape(-1, heads, head_size)
    text_values = own_text[1].reshape(-1, heads, head_size)
    cross_out = blocked(cross_q.reshape(-1, heads, head_size), text_keys, text_values).reshape(
        -1, width
    )
    own_co = lax.dynamic_index_in_dim(w_co, expert, 0, False)
    cross_proj = fold_rows(cross_out, lax.all_gather(own_co, "tok", axis=0, tiled=True))
    predicted = (hidden.astype(jnp.float32) + cross_proj).astype(jnp.bfloat16)
    term = step_coef * predicted.astype(jnp.float32)
    anchor_base = from_root(latent, "step", 0).astype(jnp.float32)
    prefix = carried_in(term, "step", lambda earlier, later: earlier + later, jnp.zeros_like(term))
    summed = prefix + term
    return (anchor_base + summed).astype(jnp.bfloat16)[None]


def solution(mesh):
    in_specs = (
        P("step", "tok", None),
        P(),
        P(),
        P(),
        P(),
        P(),
        P(None, None, "tok", None),
        P(None, "tok", None),
        P(None, None, "tok"),
        P(None, "tok", None),
        P(),
    )
    out_specs = P("step", "tok", None)
    return jax.shard_map(body, mesh=mesh, in_specs=in_specs, out_specs=out_specs, check_vma=False)
```

profile of v0, /device:TPU:0, one launch (start us, length us, event | category | flops | bytes accessed | tf_op | source)
XLA Modules:
  0.0 914.4 jit_solution(1820302305686518806)
XLA Ops:
  18.9 45.3 %all-gather.11.cloned.1.call-done = bf16[1,1152,16,216]{1,3,0,2:T(8,128)(2,1)} async-done(((bf16[1,1152,1,216]{1,3,0,2:T(8,128)(2,1)}), bf16[1,1152,16,216]{1,3,0,2:T(8,128)(2,1)}) %all-gather.11.cloned.1.call-update) | async-done | bytes 7962640 | tf_op jit(solution)/shard_map/all_gather | solution.py:75
  80.1 59.0 %all-to-all-done = bf16[512,16,1,216]{0,3,2,1:T(8,128)(2,1)} async-done(((bf16[512,16,1,216]{0,3,2,1:T(8,128)(2,1)}), bf16[512,16,1,216]{0,3,2,1:T(8,128)(2,1)}, u32[]{:S(2)}, u32[]{:S(2)}) %all-to-all-start) | async-done | bytes 3538976 | tf_op jit(solution)/shard_map/all_to_all | solution.py:79
  154.1 411.5 %while.24 = (s32[]{:T(128)}, bf16[16,512,1,72]{1,3,2,0:T(8,128)(2,1)}, bf16[16,512,1,72]{1,3,2,0:T(8,128)(2,1)}, bf16[8192,1,72]{0,2,1:T(8,128)(2,1)S(1)}, bf16[8192,1,72]{0,2,1:T(8,128)(2,1)S(1)}, /*index=5*/s32[]{:T(128)}) while((s32[]{:T(128)}, bf16[16,512,1,72]{1,3,2,0:T(8,128)(2,1)}, bf16[16,512,1,72]{1,3,2,0:T(8,128)(2,1)}, ...), condition=%wide.region_6.7_spmd, body=%wide.region_3.6_spmd.sunk | while | flops 1241586688 | bytes 52849732 | solution.py:39
  154.1 9.0 multiply_reduce_fusion.3
  163.1 8.8 fusion.84
  171.9 8.1 fusion.85
  180.0 9.0 multiply_reduce_fusion.3
  189.0 8.8 fusion.84
  197.8 8.2 fusion.85
  206.0 9.0 multiply_reduce_fusion.3
  215.0 8.6 fusion.84
  231.7 9.0 multiply_reduce_fusion.3
  240.7 8.6 fusion.84
  249.3 8.1 fusion.85
  257.4 9.0 multiply_reduce_fusion.3
  266.4 8.6 fusion.84
  275.0 8.1 fusion.85
  283.1 9.0 multiply_reduce_fusion.3
  292.1 8.6 fusion.84
  308.7 9.0 multiply_reduce_fusion.3
  317.8 8.6 fusion.84
  334.4 9.0 multiply_reduce_fusion.3
  343.4 8.6 fusion.84
  360.1 9.0 multiply_reduce_fusion.3
  369.1 8.6 fusion.84
  385.8 9.0 multiply_reduce_fusion.3
  394.8 8.6 fusion.84
  403.4 8.1 fusion.85
  411.5 9.0 multiply_reduce_fusion.3
  420.5 8.6 fusion.84
  437.2 9.0 multiply_reduce_fusion.3
  446.2 8.6 fusion.84
  454.8 8.1 fusion.85
  462.9 9.0 multiply_reduce_fusion.3
  471.9 8.6 fusion.84
  488.5 9.0 multiply_reduce_fusion.3
  497.6 8.6 fusion.84
  506.2 8.1 fusion.85
  514.2 9.0 multiply_reduce_fusion.3
  523.2 8.6 fusion.84
  539.9 9.0 multiply_reduce_fusion.3
  548.9 8.6 fusion.84
  557.5 8.1 fusion.85
  575.1 45.7 %reduce.11 = bf16[8192,72]{1,0:T(8,128)(2,1)S(1)} reduce(bf16[8192,1,1,72]{3,2,1,0:T(2,128)(2,1)} %reshape.89, bf16[]{:T(256)} %broadcast.75), dimensions={1,2}, to_apply=%reshape.89.reduce_sub_computation | reduce | bytes 2359298 | tf_op jit(solution)/shard_map/broadcast_in_dim;reshape | solution.py:51
  648.6 12.8 %reshape.94 = bf16[8192,1,1,72]{3,2,1,0:T(2,128)(2,1)} reshape(bf16[16,2,18432]{2,1,0:T(2,128)(2,1)} %all-to-all-done.1) | data formatting | bytes 2359296
  661.4 8.2 copy.28
  697.2 114.5 %all-gather.19.cloned.1.call-done = bf16[4096,1152]{1,0:T(8,128)(2,1)} async-done(((bf16[512,1152]{1,0:T(8,128)(2,1)}), bf16[4096,1152]{1,0:T(8,128)(2,1)}) %all-gather.19.cloned.1.call-update) | async-done | bytes 9437200 | tf_op jit(solution)/shard_map/all_gather | solution.py:14
  812.0 91.8 %all-reduce.2.cloned.1.call-done = bf16[512,1152]{1,0:T(8,128)(2,1)} async-done(((bf16[512,1152]{1,0:T(8,128)(2,1)}), bf16[512,1152]{1,0:T(8,128)(2,1)}) %all-reduce.2.cloned.1.call-update) | async-done | bytes 1179664 | tf_op jit(solution)/shard_map/psum | solution.py:9
  (85 shorter events, 171.3 us)
Async XLA Ops:
  6.5 4.0 copy-start
  6.5 8.2 copy-start.2
  6.5 57.6 %all-gather.11.cloned.1.call-start = ((), (), s32[]{:S(2)}) async-start(), calls=%async_computation.3 | async-start | bytes 8460288 | tf_op jit(solution)/shard_map/all_gather | solution.py:75
  10.5 4.9 copy-start.8
  11.4 660.3 %all-gather.13.cloned.1.call-start = ((), (), s32[]{:S(2)}) async-start(), calls=%async_computation.4 | async-start | bytes 2820096 | tf_op jit(solution)/shard_map/all_gather | solution.py:87
  13.1 662.7 %all-gather.15.cloned.1.call-start = ((), (), s32[]{:S(2)}) async-start(), calls=%async_computation.5 | async-start | bytes 2820096 | tf_op jit(solution)/shard_map/all_gather | solution.py:92
  73.9 5.5 copy-start.7
  73.9 65.2 %all-to-all-start = ((bf16[512,16,1,216]{0,3,2,1:T(8,128)(2,1)}), bf16[512,16,1,216]{0,3,2,1:T(8,128)(2,1)}, u32[]{:S(2)}, u32[]{:S(2)}) async-start(bf16[512,16,1,216]{0,3,2,1:T(8,128)(2,1)} %convert_bitcast_fusion), calls=%async_computation | async-start | bytes 7077888 | tf_op jit(solution)/shard_map/all_to_all | solution.py:79
  79.0 610.6 %all-gather.17.cloned.1.call-start = ((), (), s32[]{:S(2)}) async-start(), calls=%async_computation.6 | async-start | bytes 2820096 | tf_op jit(solution)/shard_map/all_gather | solution.py:103
  626.1 22.5 %all-to-all-start.1 = ((bf16[16,2,18432]{2,1,0:T(2,128)(2,1)}), bf16[16,2,18432]{2,1,0:T(2,128)(2,1)}, u32[]{:S(2)}, u32[]{:S(2)}) async-start(bf16[16,2,18432]{2,1,0:T(2,128)(2,1)} %reshape.93), calls=%async_computation.1 | async-start | bytes 2359296 | tf_op jit(solution)/shard_map/all_to_all | solution.py:80
  630.5 181.3 %all-gather.19.cloned.1.call-start = ((), (), s32[]{:S(2)}) async-start(), calls=%async_computation.7 | async-start | bytes 10616832 | tf_op jit(solution)/shard_map/all_gather | solution.py:14
  635.6 6.8 copy-start.9
  669.6 2.1 copy-start.3
  675.7 1.0 copy-start.4
  684.7 1.7 copy-start.6
  686.4 3.2 copy-start.5
  696.0 207.7 %all-reduce.2.cloned.1.call-start = ((), (), s32[]{:S(2)}) async-start(), calls=%async_computation.2 | async-start | bytes 2359296 | tf_op jit(solution)/shard_map/psum | solution.py:9
  903.8 3.5 copy-start.1
Sparse Core Ops, SparseCore 0:
  11.5 52.5 all-gather.10
  65.8 71.5 all-gather.12
  139.2 35.5 all-gather.14
  176.3 35.0 all-gather.16
  696.2 115.5 all-gather.18
  814.1 89.6 all-reduce.1
where the time goes:
time: 921 us; the launch traced here: 914 us
  waiting for transfers between devices  316 us (34%)
  matrix products  301 us (33%)
  other arithmetic  194 us (21%)
  local copies, waits for them, and re-layouts  75 us (8%)
  between operations  18.6 us (2%)
  starting transfers between devices  9.98 us (1%)
    dot_general x17, matrix products, attend(): jnp.einsum('qhc,khc->hqk', queries, keys, preferred_element_type=jnp.floa...  146 us
    reduce_sum x17, other arithmetic, attend(): total = jnp.sum(expsc, axis=-1)  140 us
    dot_general x17, matrix products, attend(): jnp.einsum('hqk,khc->qhc', expsc.astype(jnp.bfloat16), values, preferred_...  132 us
    all_gather x1, waiting for transfers between devices, carried_in(): gathered = lax.all_gather(value.astype(jnp.bfloat16), axis)  115 us
    psum x1, waiting for transfers between devices, from_root(): return lax.psum(block, axis)  91.8 us
    all_to_all x1, waiting for transfers between devices, body(): lax.all_to_all(grouped, 'tok', split_axis=1, concat_axis=0, tiled=True)  59 us
    another operation x1, other arithmetic, attend_group(): return self_attend(grouped[:, 0])[:, None]  45.7 us
    all_gather x1, waiting for transfers between devices, body(): lax.all_gather(own_qkv, 'tok', axis=1, tiled=True)  45.3 us
  transfers between devices with their start and end apart: 8, of which 5 were waited for; matrix products, arithmetic and copies ran while one was open for 61% of the time, Pallas kernels for 0%

commit v1 on v0

v1 whole, which is shorter than its diff:
```python
import functools
import math

import jax
import jax.numpy as jnp
from jax import lax
from jax.experimental import pallas as pl
from jax.experimental.pallas import tpu as pltpu
from jax.sharding import PartitionSpec as P

HEAD = 72
LANES = 128
TEXT = 300
TEXT_PAD = 384
CHUNKS = (384, 128)
SOURCES = (2, 4)
ROW_BLOCK = 512
KEY_BLOCK = 1024
VALUE = 2 * HEAD - LANES
FACTOR = math.log2(math.e) / HEAD**0.5
VMEM_LIMIT = 60 * 2**20
def link_kernel(passed, *refs):
    del passed, refs


def link(values, after):
    values = list(values)
    return pl.pallas_call(
        functools.partial(link_kernel, len(values)),
        in_specs=[pl.BlockSpec(memory_space=pl.ANY)] * (len(values) + len(after)),
        out_specs=[pl.BlockSpec(memory_space=pl.ANY)] * len(values),
        out_shape=[jax.ShapeDtypeStruct(value.shape, value.dtype) for value in values],
        input_output_aliases={index: index for index in range(len(values))},
        compiler_params=pltpu.CompilerParams(vmem_limit_bytes=VMEM_LIMIT),
        name="link",
    )(*values, *after)


def whole(array):
    return pl.BlockSpec(array.shape, lambda *_: (0,) * len(array.shape))


def project_kernel(waited, *refs):
    rows, weights, queries, keys, values = refs[waited:]
    contract = (((1,), (1,)), ((), ()))
    mixed = lax.dot_general(
        rows[...], weights[...], contract, preferred_element_type=jnp.float32
    )
    low, high = mixed[:, :LANES], mixed[:, LANES:]
    queries[...] = low.astype(jnp.bfloat16)
    lane = lax.broadcasted_iota(jnp.int32, high.shape, 1)
    values[...] = jnp.where(lane >= VALUE + HEAD, 1.0, high).astype(jnp.bfloat16)
    pad = jnp.zeros((LANES - HEAD, mixed.shape[0]), jnp.float32)
    keys[...] = jnp.concatenate([low.T[HEAD:], high.T[:VALUE], pad], 0).astype(jnp.bfloat16)


def project(tokens, weights, after):
    count, width = tokens.shape
    flat = jax.ShapeDtypeStruct((count, LANES), jnp.bfloat16)
    turned = jax.ShapeDtypeStruct((LANES, count), jnp.bfloat16)
    flat_spec = pl.BlockSpec((ROW_BLOCK, LANES), lambda i: (i, 0))
    return pl.pallas_call(
        functools.partial(project_kernel, len(after)),
        grid=(count // ROW_BLOCK,),
        in_specs=[pl.BlockSpec(memory_space=pl.ANY)] * len(after)
        + [pl.BlockSpec((ROW_BLOCK, width), lambda i: (i, 0)), whole(weights)],
        out_specs=[flat_spec, pl.BlockSpec((LANES, ROW_BLOCK), lambda i: (0, i)), flat_spec],
        out_shape=(flat, turned, flat),
        compiler_params=pltpu.CompilerParams(vmem_limit_bytes=VMEM_LIMIT),
        cost_estimate=pl.CostEstimate(
            flops=4 * count * width * LANES,
            bytes_accessed=count * width * 2 + count * 6 * LANES,
            transcendentals=0,
        ),
        name="project",
    )(*after, tokens, weights)


def attend_kernel(waited, key_chunks, carried, final, *refs):
    refs = list(refs)[waited:]
    query_ref = refs.pop(0)
    keys = refs[:key_chunks]
    values = refs[key_chunks : 2 * key_chunks]
    del refs[: 2 * key_chunks]
    state = refs.pop(0) if carried else None
    out, scores = refs
    parts = [
        (key, value, slice(start, start + KEY_BLOCK))
        for key, value in zip(keys, values)
        for start in range(0, key.shape[1], KEY_BLOCK)
    ]
    query = query_ref[...]

    def score(step):
        key, _, span = parts[step]
        return jnp.dot(query, key[:, span], preferred_element_type=jnp.float32)

    if carried:
        total = state[...]
        top = total[:, LANES - 1 :]
    else:
        total = top = None
    scores[0] = score(0)
    for step in range(len(parts)):
        if step + 1 < len(parts):
            scores[(step + 1) % 2] = score(step + 1)
        now = scores[step % 2]
        high = jnp.max(now, axis=1, keepdims=True)
        newer = high if top is None else jnp.maximum(top, high)
        weights = jnp.exp2(now * FACTOR - newer * FACTOR).astype(jnp.bfloat16)
        _, value, span = parts[step]
        part = jnp.dot(weights, value[span, :], preferred_element_type=jnp.float32)
        total = part if top is None else total * jnp.exp2((top - newer) * FACTOR) + part
        top = newer
    if final:
        turned = total.T
        done = turned[VALUE : VALUE + HEAD] / turned[VALUE + HEAD : VALUE + HEAD + 1]
        per = out.shape[2]
        for piece in range(out.shape[0]):
            out[piece] = done[:, piece * per : (piece + 1) * per].astype(jnp.bfloat16)
    else:
        lane = lax.broadcasted_iota(jnp.int32, total.shape, 1)
        out[...] = jnp.where(lane == LANES - 1, top, total)


def attend_chunk(queries, per, together, sources, state, final, after):
    count = queries.shape[0]
    block = per * together
    row_spec = pl.BlockSpec((block, LANES), lambda i: (i, 0))
    args = [*after, queries]
    in_specs = [pl.BlockSpec(memory_space=pl.ANY)] * len(after) + [row_spec]
    for index in (1, 2):
        args += [chunk[index] for chunk in sources]
        in_specs += [whole(chunk[index]) for chunk in sources]
    if state is not None:
        args.append(state)
        in_specs.append(row_spec)
    if final:
        out_shape = jax.ShapeDtypeStruct((count // per, HEAD, per), jnp.bfloat16)
        out_spec = pl.BlockSpec((together, HEAD, per), lambda i: (i, 0, 0))
    else:
        out_shape = jax.ShapeDtypeStruct((count, LANES), jnp.float32)
        out_spec = row_spec
    pairs = count * sum(chunk[1].shape[1] for chunk in sources)
    return pl.pallas_call(
        functools.partial(attend_kernel, len(after), len(sources), state is not None, final),
        grid=(count // block,),
        in_specs=in_specs,
        out_specs=out_spec,
        scratch_shapes=[pltpu.VMEM((2, block, KEY_BLOCK), jnp.float32)],
        out_shape=out_shape,
        compiler_params=pltpu.CompilerParams(vmem_limit_bytes=VMEM_LIMIT),
        cost_estimate=pl.CostEstimate(
            flops=4 * pairs * LANES * 2, bytes_accessed=4 * 2**20, transcendentals=pairs
        ),
        name="self_attend",
    )(*args)


def self_attend(normed, weights, early):
    chunks, states, previous, start = [], [], [], 0
    held = None
    for chunk, per in enumerate(CHUNKS):
        own = normed[start : start + per]
        start += per
        if held is not None:
            own = link([own], [held])[0]
        held = lax.all_gather(own, "tok", axis=0, tiled=True)
        chunks.append([held])
    for chunk, per in enumerate(CHUNKS):
        last = chunk + 1 == len(CHUNKS)
        chunks[chunk] = project(chunks[chunk][0], weights, previous + early[chunk])
        for earlier in range(chunk + 1):
            before = states[earlier] if earlier < chunk else None
            keys = chunks[chunk : chunk + 1] if earlier < chunk else chunks[: chunk + 1]
            result = attend_chunk(
                chunks[earlier][0], CHUNKS[earlier], SOURCES[earlier], keys, before, last, previous
            )
            previous = [result]
            states[earlier : earlier + 1] = [result]
    return states, chunks


def finish_kernel(parts, *refs):
    turned, (latent, gate, weights, keys, values, out, cross) = refs[:parts], refs[parts:]
    width = latent.shape[1]

    def weight(index):
        return weights[:, index].astype(jnp.float32).reshape(width, width).astype(jnp.bfloat16)

    attended = jnp.concatenate([part[...].astype(jnp.float32) for part in turned], 1)
    attended = attended.T.astype(jnp.bfloat16)
    projected = jnp.dot(attended, weight(0), preferred_element_type=jnp.float32)
    hidden = (latent[...].astype(jnp.float32) + gate[...] * projected).astype(jnp.bfloat16)
    queries = lax.dot_general(
        weight(1), hidden, (((1,), (1,)), ((), ())), preferred_element_type=jnp.float32
    )
    for head in range(width // HEAD):
        rows = slice(head * HEAD, (head + 1) * HEAD)
        scores = jnp.dot(
            keys[head], queries[rows].astype(jnp.bfloat16), preferred_element_type=jnp.float32
        )
        row = lax.broadcasted_iota(jnp.int32, scores.shape, 0)
        scores = jnp.where(row < TEXT, scores, -jnp.inf)
        high = jnp.max(scores, axis=0, keepdims=True)
        exps = jnp.exp2((scores - high) * FACTOR)
        total = jnp.sum(exps, axis=0, keepdims=True)
        result = jnp.dot(
            values[head], exps.astype(jnp.bfloat16), preferred_element_type=jnp.float32
        )
        cross[rows, :] = result / total
    crossed = cross[...].T.astype(jnp.bfloat16)
    out[...] = (
        hidden.astype(jnp.float32)
        + jnp.dot(crossed, weight(2), preferred_element_type=jnp.float32)
    ).astype(jnp.bfloat16)


def finish(turned, latent, gate, weights, keys, values):
    count, width = latent.shape
    args = (*turned, latent, gate, weights, keys, values)
    return pl.pallas_call(
        functools.partial(finish_kernel, len(turned)),
        grid=(1,),
        in_specs=[whole(arg) for arg in args],
        out_specs=whole(latent),
        out_shape=jax.ShapeDtypeStruct((count, width), jnp.bfloat16),
        scratch_shapes=[pltpu.VMEM((width, count), jnp.float32)],
        compiler_params=pltpu.CompilerParams(vmem_limit_bytes=VMEM_LIMIT),
        cost_estimate=pl.CostEstimate(
            flops=10 * count * width * width, bytes_accessed=10 * 2**20, transcendentals=0
        ),
        name="finish",
    )(*args)


def scan_kernel(coefs, first, everyone, out):
    running = first[...].astype(jnp.float32)
    for step in range(everyone.shape[0]):
        running = running + coefs[step] * everyone[step].astype(jnp.float32)
        out[step] = running.astype(jnp.bfloat16)


def scan(coefs, first, everyone):
    return pl.pallas_call(
        scan_kernel,
        grid_spec=pltpu.PrefetchScalarGridSpec(
            num_scalar_prefetch=1,
            grid=(1,),
            in_specs=[whole(first), whole(everyone)],
            out_specs=whole(everyone),
        ),
        out_shape=jax.ShapeDtypeStruct(everyone.shape, jnp.bfloat16),
        compiler_params=pltpu.CompilerParams(vmem_limit_bytes=VMEM_LIMIT),
        name="scan",
    )(coefs, first, everyone)


def body(latents, timesteps, experts, offset, modulation, coef, w_qkv, w_o, w_cq, w_co, text_kv):
    step_index = lax.axis_index("step")
    steps = lax.axis_size("step")
    position = offset[0] + step_index
    entry = lax.dynamic_index_in_dim(timesteps, position, 0, False)
    expert = lax.dynamic_index_in_dim(experts, position, 0, False)
    modulate = lax.dynamic_index_in_dim(modulation, entry, 0, False)
    latent = latents[0]
    count, width = latent.shape
    heads = width // HEAD
    flat = latent.astype(jnp.float32)
    mean = jnp.mean(flat, axis=1, keepdims=True)
    var = jnp.mean((flat - mean) ** 2, axis=1, keepdims=True)
    normed = ((flat - mean) * lax.rsqrt(var + 1e-06) * (1.0 + modulate[1]) + modulate[0]).astype(
        jnp.bfloat16
    )
    own_qkv = jnp.swapaxes(lax.dynamic_index_in_dim(w_qkv, expert, 0, False)[:, 0, :], 0, 1)
    w_mixed = jnp.pad(own_qkv, ((0, 2 * LANES - 3 * HEAD), (0, 0)))

    def over_steps(value):
        shaped = value.reshape(steps, -1, width)
        return lax.all_to_all(shaped, "step", split_axis=0, concat_axis=0, tiled=True)

    first = over_steps(latent)[0]
    own_text = lax.dynamic_index_in_dim(text_kv, expert, 0, False).reshape(2, TEXT, heads, HEAD)
    text_keys = jnp.pad(
        jnp.transpose(own_text[0], (1, 0, 2)), ((0, 0), (0, TEXT_PAD - TEXT), (0, 0))
    )
    text_values = jnp.pad(
        jnp.transpose(own_text[1], (1, 2, 0)), ((0, 0), (0, 0), (0, TEXT_PAD - TEXT))
    )
    first, text_keys, text_values = link([first, text_keys, text_values], [])
    own_weights = jnp.stack(
        [
            lax.dynamic_index_in_dim(w_o, expert, 0, False),
            jnp.swapaxes(lax.dynamic_index_in_dim(w_cq, expert, 0, False), 0, 1),
            lax.dynamic_index_in_dim(w_co, expert, 0, False),
        ]
    )
    heads_out, chunks = self_attend(
        normed, w_mixed, ([first], [text_keys, text_values, own_weights])
    )
    all_weights = lax.all_gather(
        link([own_weights], [chunks[0][0]])[0], "tok", axis=0, tiled=False
    )

    def returned(value):
        back = lax.all_to_all(value, "tok", split_axis=0, concat_axis=0, tiled=True)
        return back.reshape(width, -1)

    turned = [returned(heads_out[0])]
    turned.append(returned(link([heads_out[1]], turned)[0]))
    predicted = finish(turned, latent, modulate[2][None], all_weights, text_keys, text_values)
    coefs = jnp.take(coef, lax.dynamic_slice_in_dim(timesteps, offset[0], steps))
    return over_steps(scan(coefs, first, over_steps(predicted))).reshape(1, count, width)


def solution(mesh):
    in_specs = (
        P("step", "tok", None),
        P(),
        P(),
        P(),
        P(),
        P(),
        P(None, None, "tok", None),
        P(None, "tok", None),
        P(None, None, "tok"),
        P(None, "tok", None),
        P(),
    )
    out_specs = P("step", "tok", None)
    return jax.shard_map(body, mesh=mesh, in_specs=in_specs, out_specs=out_specs, check_vma=False)
```

time: 921 us -> 348 us (0.38)
  matrix products: 301 us -> 0 us
  waiting for transfers between devices: 316 us -> 106 us
  other arithmetic: 194 us -> 8 us
  Pallas kernels: 0 us -> 138 us
  local copies, waits for them, and re-layouts: 75 us -> 26.4 us
  blocking collectives: 0 us -> 35.7 us
    dot_general x37 -> x0, matrix products: 293 us -> none  [the longest x17 146 us: attend(): jnp.einsum('qhc,khc->hqk', queries, keys, preferred_element_type=jnp.floa...]
    reduce_sum x17 -> x0, other arithmetic: 140 us -> none  [attend(): total = jnp.sum(expsc, axis=-1)]
    pallas_call x0 -> x11, Pallas kernels: none -> 138 us  [the longest x3 99.2 us: attend_chunk(): pl.pallas_call(functools.partial(attend_kernel, len(after), len(sources),...]
    psum x1 -> x0, waiting for transfers between devices: 91.8 us -> none  [from_root(): return lax.psum(block, axis)]
    all_gather x5 -> x3, waiting for transfers between devices: 160 us -> 81.1 us  [the longest x2 81.1 us: self_attend(): held = lax.all_gather(own, 'tok', axis=0, tiled=True)]
    another operation x1, other arithmetic: 45.7 us -> 0.85 us  [body(): jnp.stack([lax.dynamic_index_in_dim(w_o, expert, 0, False), jnp.swapaxes(...]
    all_to_all x2 -> x3, waiting for transfers between devices: 64.4 us -> 24.3 us  [the longest x2 24.2 us: over_steps(): lax.all_to_all(shaped, 'step', split_axis=0, concat_axis=0, tiled=True)]
    all_to_all x0 -> x2, blocking collectives: none -> 35.7 us  [the longest x1 21.6 us: over_steps(): lax.all_to_all(shaped, 'step', split_axis=0, concat_axis=0, tiled=True)]
  transfers between devices with their start and end apart: 8 -> 6, of which waited for: 5 -> 4; matrix products, arithmetic and copies ran while one was open for 61% -> 6% of each run, Pallas kernels for 0% -> 33%
where the time goes in v1:
time: 348 us; the launch traced here: 347 us
  Pallas kernels  138 us (40%)
  waiting for transfers between devices  106 us (30%)
  blocking collectives  35.7 us (10%)
  local copies, waits for them, and re-layouts  26.4 us (8%)
  between operations  17.8 us (5%)
  starting transfers between devices  14.2 us (4%)
  other arithmetic  8 us (2%)
    pallas_call x3, Pallas kernels, attend_chunk(): pl.pallas_call(functools.partial(attend_kernel, len(after), len(sources),...  99.2 us
    all_gather x2, waiting for transfers between devices, self_attend(): held = lax.all_gather(own, 'tok', axis=0, tiled=True)  81.1 us
    all_to_all x2, waiting for transfers between devices, over_steps(): lax.all_to_all(shaped, 'step', split_axis=0, concat_axis=0, tiled=True)  24.2 us
    all_to_all x1, blocking collectives, over_steps(): lax.all_to_all(shaped, 'step', split_axis=0, concat_axis=0, tiled=True)  21.6 us
    pallas_call x2, Pallas kernels, project(): pl.pallas_call(functools.partial(project_kernel, len(after)), grid=(count...  19.4 us
    pallas_call x1, Pallas kernels, finish(): pl.pallas_call(functools.partial(finish_kernel, len(turned)), grid=(1,),...  16.3 us
    all_to_all x1, blocking collectives, returned(): back = lax.all_to_all(value, 'tok', split_axis=0, concat_axis=0, tiled=True)  14.1 us
    all_to_all x2, starting transfers between devices, over_steps(): lax.all_to_all(shaped, 'step', split_axis=0, concat_axis=0, tiled=True)  10.5 us
  transfers between devices with their start and end apart: 6, of which 4 were waited for; matrix products, arithmetic and copies ran while one was open for 6% of the time, Pallas kernels for 33%

profile of v1, /device:TPU:0, one launch (start us, length us, event | category | flops | bytes accessed | tf_op | source)
XLA Modules:
  0.0 346.5 jit_solution(1510637599515893612)
XLA Ops:
  6.5 0.0 copy-start
  6.5 0.0 all-gather.5.cloned.1.call-start
  7.3 1.2 dynamic_slice.36
  9.8 1.5 convert_reduce_fusion
  11.3 1.7 fusion.2
  13.7 1.4 fusion.6
  15.1 1.8 fusion.5
  16.9 1.0 slice.43
  17.9 0.0 all-gather.5.cloned.1.call-update
  17.9 0.0 all-gather.7.cloned.1.call-start
  18.0 0.7 slice.44.refs_0_
  18.7 81.1 %all-gather.5.cloned.1.call-done.refs_1_ = bf16[6144,1152]{1,0:T(8,128)(2,1)} async-done(((bf16[384,1152]{1,0:T(8,128)(2,1)}), bf16[6144,1152]{1,0:T(8,128)(2,1)}) %all-gather.5.cloned.1.call-update) | async-done | bytes 14155792 | tf_op jit(solution)/shard_map/all_gather | solution.py:168
  99.8 0.0 all-gather.7.cloned.1.call-update
  99.8 6.9 %all-to-all-start = ((bf16[8,64,1152]{2,1,0:T(8,128)(2,1)}), bf16[8,64,1152]{2,1,0:T(8,128)(2,1)}, u32[]{:S(2)}, u32[]{:S(2)}) async-start(bf16[8,64,1152]{2,1,0:T(8,128)(2,1)} %bitcast.1), calls=%async_computation | async-start | bytes 2359296 | tf_op jit(solution)/shard_map/all_to_all | solution.py:280
  106.7 0.6 dynamic_slice.34
  109.2 5.1 %constant_dynamic-slice_fusion.3 = (bf16[1,1,300,1152]{3,1,2,0:T(2,128)(2,1)S(1)}, bf16[1,1,300,1152]{3,1,2,0:T(2,128)(2,1)}) fusion(bf16[2,2,300,1152]{3,1,2,0:T(2,128)(2,1)} %param.21, s32[]{:T(128)S(6)} %select_n.36, s32[]{:T(128)S(6)} %add.86), kind=kLoop, calls=%fused_computation.22 | loop fusion | bytes 2764808 | tf_op jit(solution)/shard_map/slice | solution.py:288
  114.3 3.6 %copy.24 = bf16[1,1,300,1152]{2,3,1,0:T(8,128)(2,1)S(1)} copy(bf16[1,1,300,1152]{3,1,2,0:T(2,128)(2,1)} %get-tuple-element.26) | data formatting | bytes 1382400
  117.9 1.5 copy.22
  119.4 2.1 copy.25
  121.5 2.9 pad.12.refs_1_
  124.4 1.1 pad.13.refs_2_
  125.6 0.9 pad.14.refs_2_.refs_5_
  126.4 0.1 copy-done.5
  126.5 0.3 copy-done.6
  126.8 0.8 pad_maximum_fusion.refs_3_.refs_0_
  127.7 7.3 %all-to-all-done = bf16[8,64,1152]{2,1,0:T(8,128)(2,1)} async-done(((bf16[8,64,1152]{2,1,0:T(8,128)(2,1)}), bf16[8,64,1152]{2,1,0:T(8,128)(2,1)}, u32[]{:S(2)}, u32[]{:S(2)}) %all-to-all-start) | async-done | bytes 1179680 | tf_op jit(solution)/shard_map/all_to_all | solution.py:280
  134.9 1.6 slice_bitcast_fusion.refs_0_
  136.5 13.9 %project.2 = (bf16[6144,128]{1,0:T(8,128)(2,1)}, bf16[128,6144]{1,0:T(8,128)(2,1)}, bf16[6144,128]{1,0:T(8,128)(2,1)}) custom-call(bf16[64,1152]{1,0:T(8,128)(2,1)} %get-tuple-element.14.refs_0_.first, bf16[6144,1152]{1,0:T(8,128)(2,1)} %all-gather.5.cloned.1.call-done.refs_1_, bf16[256,1152]{1,0:T(8,128)(2,1)} %pad.14.refs_2_.refs_5_), custom_call_target="tpu_custom_call" | custom-call | flops 3623878656 | bytes 18874368 | tf_op jit(solution)/shard_map/project/pallas_call | solution.py:62
  150.4 51.0 %self_attend.3.refs_0_.refs_4_ = f32[6144,128]{1,0:T(8,128)} custom-call(bf16[6144,128]{1,0:T(8,128)(2,1)} %get-tuple-element.15.refs_0_.refs_1_, bf16[128,6144]{1,0:T(8,128)(2,1)} %get-tuple-element.16.refs_1_.refs_2_, bf16[6144,128]{1,0:T(8,128)(2,1)} %get-tuple-element.17.refs_2_.refs_4_), custom_call_target="tpu_custom_call" | custom-call | flops 38654705664 | bytes 4194304 | tf_op jit(solution)/shard_map/self_attend/pallas_call | solution.py:145
  201.5 5.5 %project.3 = (bf16[2048,128]{1,0:T(8,128)(2,1)}, bf16[128,2048]{1,0:T(8,128)(2,1)}, bf16[2048,128]{1,0:T(8,128)(2,1)}) custom-call(f32[6144,128]{1,0:T(8,128)} %self_attend.3.refs_0_.refs_4_, bf16[16,384,72]{2,1,0:T(8,128)(2,1)} %get-tuple-element.18.refs_1_.refs_5_, bf16[16,72,384]{2,1,0:T(8,128)(2,1)} %get-tuple-element.19.refs_2_.refs_6_, ...), custom_call_target="tpu_custom_call" | custom-call | flops 1207959552 | bytes 6291456 | tf_op jit(solution)/shard_map/project/pallas_call | solution.py:62
  207.0 0.0 all-gather.9.cloned.1.call-start
  207.0 0.7 all-gather.9.cloned.1.call-update
  207.7 23.8 %self_attend.4.refs_0_ = bf16[16,72,384]{2,1,0:T(8,128)(2,1)} custom-call(f32[6144,128]{1,0:T(8,128)} %self_attend.3.refs_0_.refs_4_, bf16[6144,128]{1,0:T(8,128)(2,1)} %get-tuple-element.15.refs_0_.refs_1_, bf16[128,2048]{1,0:T(8,128)(2,1)} %get-tuple-element.20.refs_2_.refs_3_, bf16[2048,128]{1,0:T(8,128)(2,1)} %get-tuple-element.21.refs_3_.refs_5_, ...), custom_call_target="tpu_custom_call" | custom-call | flops 12884901888 | bytes 4194304 | tf_op jit(solution)/shard_map/self_attend/pallas_call | solution.py:145
  231.5 3.6 %all-to-all-start.1 = ((bf16[16,72,384]{2,1,0:T(8,128)(2,1)}), bf16[16,72,384]{2,1,0:T(8,128)(2,1)S(1)}, u32[]{:S(2)}, u32[]{:S(2)}) async-start(bf16[16,72,384]{2,1,0:T(8,128)(2,1)} %self_attend.4.refs_0_), calls=%async_computation.1 | async-start | bytes 1769472 | tf_op jit(solution)/shard_map/all_to_all | solution.py:306
  235.1 24.4 %self_attend.5.refs_0_ = bf16[16,72,128]{2,1,0:T(8,128)(2,1)} custom-call(bf16[16,72,384]{2,1,0:T(8,128)(2,1)} %self_attend.4.refs_0_, bf16[2048,128]{1,0:T(8,128)(2,1)} %get-tuple-element.22.refs_1_, bf16[128,6144]{1,0:T(8,128)(2,1)} %get-tuple-element.16.refs_1_.refs_2_, bf16[128,2048]{1,0:T(8,128)(2,1)} %get-tuple-element.20.refs_2_.refs_3_, ...), custom_call_target="tpu_custom_call" | custom-call | flops 17179869184 | bytes 4194304 | tf_op jit(solution)/shard_map/self_attend/pallas_call | solution.py:145
  259.5 0.1 all-to-all-done.1
  259.6 1.0 copy-done.3
  260.6 14.1 %all_to_all.25 = bf16[16,72,128]{2,1,0:T(8,128)(2,1)} all-to-all(bf16[16,72,128]{2,1,0:T(8,128)(2,1)} %link.6), channel_id=1, replica_groups=mesh['step'=8,'tok'=16] {'tok'}, dimensions={0} | all-to-all | bytes 589824 | tf_op jit(solution)/shard_map/all_to_all | solution.py:306
  274.7 16.3 %finish.1 = bf16[512,1152]{1,0:T(8,128)(2,1)} custom-call(bf16[1152,384]{1,0:T(8,128)(2,1)} %bitcast.41, bf16[1152,128]{1,0:T(8,128)(2,1)} %bitcast.43, bf16[512,1152]{1,0:T(8,128)(2,1)} %bitcast.8.refs_2_, f32[1,1152]{1,0:T(1,128)} %get-tuple-element.27.refs_3_, bf16[16,3,72,1152]{3,2,1,0:T(8,128)(2,1)} %bitcast.44, ...), custom_call_target="tpu_custom_call" | custom-call | flops 6794772480 | bytes 10485760 | tf_op jit(solution)/shard_map/finish/pallas_call | solution.py:222
  290.9 3.7 %all-to-all-start.3 = ((bf16[8,64,1152]{2,1,0:T(8,128)(2,1)}), bf16[8,64,1152]{2,1,0:T(8,128)(2,1)S(1)}, u32[]{:S(2)}, u32[]{:S(2)}) async-start(bf16[8,64,1152]{2,1,0:T(8,128)(2,1)} %bitcast.42), calls=%async_computation.3 | async-start | bytes 2359296 | tf_op jit(solution)/shard_map/all_to_all | solution.py:280
  294.6 0.1 compare_select_fusion
  294.7 0.6 gather_fusion
  295.4 0.7 and_select_fusion.coefs
  296.0 17.0 %all-to-all-done.3.everyone = bf16[8,64,1152]{2,1,0:T(8,128)(2,1)S(1)} async-done(((bf16[8,64,1152]{2,1,0:T(8,128)(2,1)}), bf16[8,64,1152]{2,1,0:T(8,128)(2,1)S(1)}, u32[]{:S(2)}, u32[]{:S(2)}) %all-to-all-start.3) | async-done | bytes 1179680 | tf_op jit(solution)/shard_map/all_to_all | solution.py:280
  313.0 1.0 copy-done.2
  314.0 3.4 scan.1
  317.4 21.6 %all_to_all.26 = bf16[8,64,1152]{2,1,0:T(8,128)(2,1)S(1)} all-to-all(bf16[8,64,1152]{2,1,0:T(8,128)(2,1)} %scan.1), channel_id=1, replica_groups=mesh['step'=8,'tok'=16] {'step'}, dimensions={0} | all-to-all | bytes 2359296 | tf_op jit(solution)/shard_map/all_to_all | solution.py:280
  339.0 1.0 copy.34
  (25 shorter events, 0.1 us)
Async XLA Ops:
  6.5 119.0 %copy-start = (bf16[2,1152,1,216]{1,3,2,0:T(8,128)(2,1)S(1)}, bf16[2,1152,1,216]{1,3,2,0:T(8,128)(2,1)}, u32[]{:S(2)}) copy-start(bf16[2,1152,1,216]{1,3,2,0:T(8,128)(2,1)} %param.17) | copy-start | bytes 2985988
  6.5 93.2 %all-gather.5.cloned.1.call-start = ((), (), s32[]{:S(2)}) async-start(), calls=%async_computation.5 | async-start | bytes 15040512 | tf_op jit(solution)/shard_map/all_gather | solution.py:168
  17.9 183.6 %all-gather.7.cloned.1.call-start = ((), (), s32[]{:S(2)}) async-start(), calls=%async_computation.6 | async-start | bytes 5013504 | tf_op jit(solution)/shard_map/all_gather | solution.py:168
  99.8 6.9 %copy-start.8 = (s32[32]{0:T(128)S(1)}, s32[32]{0:T(128)}, u32[]{:S(2)}) copy-start(s32[32]{0:T(128)} %param.13) | copy-start | bytes 388
  99.8 35.1 %all-to-all-start = ((bf16[8,64,1152]{2,1,0:T(8,128)(2,1)}), bf16[8,64,1152]{2,1,0:T(8,128)(2,1)}, u32[]{:S(2)}, u32[]{:S(2)}) async-start(bf16[8,64,1152]{2,1,0:T(8,128)(2,1)} %bitcast.1), calls=%async_computation | async-start | bytes 2359296 | tf_op jit(solution)/shard_map/all_to_all | solution.py:280
  124.4 2.0 copy-start.4
  125.5 1.0 copy-start.5
  125.5 1.3 copy-start.6
  207.0 67.7 %all-gather.9.cloned.1.call-start = ((), (), s32[]{:S(2)}) async-start(), calls=%async_computation.7 | async-start | bytes 8460288 | tf_op jit(solution)/shard_map/all_gather | solution.py:301
  231.5 28.1 %all-to-all-start.1 = ((bf16[16,72,384]{2,1,0:T(8,128)(2,1)}), bf16[16,72,384]{2,1,0:T(8,128)(2,1)S(1)}, u32[]{:S(2)}, u32[]{:S(2)}) async-start(bf16[16,72,384]{2,1,0:T(8,128)(2,1)} %self_attend.4.refs_0_), calls=%async_computation.1 | async-start | bytes 1769472 | tf_op jit(solution)/shard_map/all_to_all | solution.py:306
  259.6 1.0 copy-start.3
  290.9 3.7 %copy-start.7 = (s32[32]{0:T(128)S(1)}, s32[32]{0:T(128)}, u32[]{:S(2)}) copy-start(s32[32]{0:T(128)} %param.12) | copy-start | bytes 388
  290.9 3.8 %copy-start.1 = (f32[64]{0:T(128)S(1)}, f32[64]{0:T(128)}, u32[]{:S(2)}) copy-start(f32[64]{0:T(128)} %param.16) | copy-start | bytes 772
  290.9 22.1 %all-to-all-start.3 = ((bf16[8,64,1152]{2,1,0:T(8,128)(2,1)}), bf16[8,64,1152]{2,1,0:T(8,128)(2,1)S(1)}, u32[]{:S(2)}, u32[]{:S(2)}) async-start(bf16[8,64,1152]{2,1,0:T(8,128)(2,1)} %bitcast.42), calls=%async_computation.3 | async-start | bytes 2359296 | tf_op jit(solution)/shard_map/all_to_all | solution.py:280
  313.0 1.0 copy-start.2
Sparse Core Ops, SparseCore 0:
  18.0 81.7 all-gather.4
  101.5 45.6 all-gather.6
  209.5 55.3 all-gather.8

commit v2 on v1

--- a/solution.py
+++ b/solution.py
@@ -13,9 +13,10 @@
 TEXT = 300
 TEXT_PAD = 384
 CHUNKS = (384, 128)
-SOURCES = (2, 4)
-ROW_BLOCK = 512
+SOURCES = (2, 8)
+ROW_BLOCK = 1024
 KEY_BLOCK = 1024
+HALVES = 2
 VALUE = 2 * HEAD - LANES
 FACTOR = math.log2(math.e) / HEAD**0.5
 VMEM_LIMIT = 60 * 2**20
@@ -42,10 +43,7 @@
 
 def project_kernel(waited, *refs):
     rows, weights, queries, keys, values = refs[waited:]
-    contract = (((1,), (1,)), ((), ()))
-    mixed = lax.dot_general(
-        rows[...], weights[...], contract, preferred_element_type=jnp.float32
-    )
+    mixed = jnp.dot(rows[...], weights[...], preferred_element_type=jnp.float32)
     low, high = mixed[:, :LANES], mixed[:, LANES:]
     queries[...] = low.astype(jnp.bfloat16)
     lane = lax.broadcasted_iota(jnp.int32, high.shape, 1)
@@ -89,38 +87,44 @@
         for key, value in zip(keys, values)
         for start in range(0, key.shape[1], KEY_BLOCK)
     ]
-    query = query_ref[...]
-
-    def score(step):
+    rows = query_ref.shape[0] // HALVES
+    spans = [slice(half * rows, (half + 1) * rows) for half in range(HALVES)]
+    units = [(half, step) for step in range(len(parts)) for half in range(HALVES)]
+
+    def score(unit):
+        half, step = unit
         key, _, span = parts[step]
-        return jnp.dot(query, key[:, span], preferred_element_type=jnp.float32)
-
-    if carried:
-        total = state[...]
-        top = total[:, LANES - 1 :]
-    else:
-        total = top = None
-    scores[0] = score(0)
-    for step in range(len(parts)):
-        if step + 1 < len(parts):
-            scores[(step + 1) % 2] = score(step + 1)
-        now = scores[step % 2]
+        return jnp.dot(
+            query_ref[spans[half], :], key[:, span], preferred_element_type=jnp.float32
+        )
+
+    totals = [state[span, :] if carried else None for span in spans]
+    tops = [total[:, LANES - 1 :] if carried else None for total in totals]
+    scores[0] = score(units[0])
+    for index, (half, step) in enumerate(units):
+        if index + 1 < len(units):
+            scores[(index + 1) % 2] = score(units[index + 1])
+        now = scores[index % 2]
+        top, total = tops[half], totals[half]
         high = jnp.max(now, axis=1, keepdims=True)
         newer = high if top is None else jnp.maximum(top, high)
         weights = jnp.exp2(now * FACTOR - newer * FACTOR).astype(jnp.bfloat16)
         _, value, span = parts[step]
         part = jnp.dot(weights, value[span, :], preferred_element_type=jnp.float32)
-        total = part if top is None else total * jnp.exp2((top - newer) * FACTOR) + part
-        top = newer
-    if final:
-        turned = total.T
-        done = turned[VALUE : VALUE + HEAD] / turned[VALUE + HEAD : VALUE + HEAD + 1]
-        per = out.shape[2]
-        for piece in range(out.shape[0]):
-            out[piece] = done[:, piece * per : (piece + 1) * per].astype(jnp.bfloat16)
-    else:
-        lane = lax.broadcasted_iota(jnp.int32, total.shape, 1)
-        out[...] = jnp.where(lane == LANES - 1, top, total)
+        totals[half] = part if top is None else total * jnp.exp2((top - newer) * FACTOR) + part
+        tops[half] = newer
+    for half, (total, top) in enumerate(zip(totals, tops)):
+        if final:
+            turned = total.T
+            done = turned[VALUE : VALUE + HEAD] / turned[VALUE + HEAD : VALUE + HEAD + 1]
+            per = out.shape[2]
+            for piece in range(rows // per):
+                out[half * (rows // per) + piece] = done[
+                    :, piece * per : (piece + 1) * per
+                ].astype(jnp.bfloat16)
+        else:
+            lane = lax.broadcasted_iota(jnp.int32, total.shape, 1)
+            out[spans[half], :] = jnp.where(lane == LANES - 1, top, total)
 
 
 def attend_chunk(queries, per, together, sources, state, final, after):
@@ -147,7 +151,7 @@
         grid=(count // block,),
         in_specs=in_specs,
         out_specs=out_spec,
-        scratch_shapes=[pltpu.VMEM((2, block, KEY_BLOCK), jnp.float32)],
+        scratch_shapes=[pltpu.VMEM((2, block // HALVES, KEY_BLOCK), jnp.float32)],
         out_shape=out_shape,
         compiler_params=pltpu.CompilerParams(vmem_limit_bytes=VMEM_LIMIT),
         cost_estimate=pl.CostEstimate(
@@ -164,12 +168,12 @@
         own = normed[start : start + per]
         start += per
         if held is not None:
-            own = link([own], [held])[0]
+            own = link([own], [held] + early[chunk])[0]
         held = lax.all_gather(own, "tok", axis=0, tiled=True)
         chunks.append([held])
     for chunk, per in enumerate(CHUNKS):
         last = chunk + 1 == len(CHUNKS)
-        chunks[chunk] = project(chunks[chunk][0], weights, previous + early[chunk])
+        chunks[chunk] = project(chunks[chunk][0], weights, previous)
         for earlier in range(chunk + 1):
             before = states[earlier] if earlier < chunk else None
             keys = chunks[chunk : chunk + 1] if earlier < chunk else chunks[: chunk + 1]
@@ -272,8 +276,8 @@
     normed = ((flat - mean) * lax.rsqrt(var + 1e-06) * (1.0 + modulate[1]) + modulate[0]).astype(
         jnp.bfloat16
     )
-    own_qkv = jnp.swapaxes(lax.dynamic_index_in_dim(w_qkv, expert, 0, False)[:, 0, :], 0, 1)
-    w_mixed = jnp.pad(own_qkv, ((0, 2 * LANES - 3 * HEAD), (0, 0)))
+    own_qkv = lax.dynamic_index_in_dim(w_qkv, expert, 0, False)[:, 0, :]
+    w_mixed = jnp.pad(own_qkv, ((0, 0), (0, 2 * LANES - 3 * HEAD)))
 
     def over_steps(value):
         shaped = value.reshape(steps, -1, width)
@@ -296,7 +300,7 @@
         ]
     )
     heads_out, chunks = self_attend(
-        normed, w_mixed, ([first], [text_keys, text_values, own_weights])
+        normed, w_mixed, ([], [first, text_keys, text_values, own_weights, w_mixed])
     )
     all_weights = lax.all_gather(
         link([own_weights], [chunks[0][0]])[0], "tok", axis=0, tiled=False

time: 348 us -> 321 us (0.922); the launches traced: 347 us -> 315 us
  waiting for transfers between devices: 106 us -> 75.6 us
  Pallas kernels: 138 us -> 130 us
  starting transfers between devices: 14.2 us -> 20.9 us
    all_gather x2, waiting for transfers between devices: 81.1 us -> 51.3 us  [self_attend(): held = lax.all_gather(own, 'tok', axis=0, tiled=True)]
    all_to_all x2, starting transfers between devices: 10.5 us -> 15.1 us  [over_steps(): lax.all_to_all(shaped, 'step', split_axis=0, concat_axis=0, tiled=True)]
    pallas_call x2, Pallas kernels: 19.4 us -> 15 us  [project(): pl.pallas_call(functools.partial(project_kernel, len(after)), grid=(count...]
    pallas_call x3, Pallas kernels: 99.2 us -> 95.7 us  [attend_chunk(): pl.pallas_call(functools.partial(attend_kernel, len(after), len(sources),...]
  transfers between devices with their start and end apart: 6 -> 6, of which waited for: 4 -> 3; matrix products, arithmetic and copies ran while one was open for 6% -> 7% of each run, Pallas kernels for 33% -> 35%
where the time goes in v2:
time: 321 us; the launch traced here: 315 us
  Pallas kernels  130 us (40%)
  waiting for transfers between devices  75.6 us (24%)
  blocking collectives  36 us (11%)
  local copies, waits for them, and re-layouts  26.3 us (8%)
  starting transfers between devices  20.9 us (7%)
  between operations  18.1 us (6%)
  other arithmetic  8.01 us (2%)
    pallas_call x3, Pallas kernels, attend_chunk(): pl.pallas_call(functools.partial(attend_kernel, len(after), len(sources),...  95.7 us
    all_gather x2, waiting for transfers between devices, self_attend(): held = lax.all_gather(own, 'tok', axis=0, tiled=True)  51.3 us
    all_to_all x2, waiting for transfers between devices, over_steps(): lax.all_to_all(shaped, 'step', split_axis=0, concat_axis=0, tiled=True)  24.2 us
    all_to_all x1, blocking collectives, over_steps(): lax.all_to_all(shaped, 'step', split_axis=0, concat_axis=0, tiled=True)  21.5 us
    pallas_call x1, Pallas kernels, finish(): pl.pallas_call(functools.partial(finish_kernel, len(turned)), grid=(1,),...  16.3 us
    all_to_all x2, starting transfers between devices, over_steps(): lax.all_to_all(shaped, 'step', split_axis=0, concat_axis=0, tiled=True)  15.1 us
    pallas_call x2, Pallas kernels, project(): pl.pallas_call(functools.partial(project_kernel, len(after)), grid=(count...  15 us
    all_to_all x1, blocking collectives, returned(): back = lax.all_to_all(value, 'tok', split_axis=0, concat_axis=0, tiled=True)  14.5 us
  transfers between devices with their start and end apart: 6, of which 3 were waited for; matrix products, arithmetic and copies ran while one was open for 7% of the time, Pallas kernels for 35%

profile of v2, /device:TPU:0, one launch (start us, length us, event | category | flops | bytes accessed | tf_op | source)
XLA Modules:
  0.0 315.2 jit_solution(4159303829107583785)
XLA Ops:
  7.3 1.2 dynamic_slice.36
  9.8 1.5 convert_reduce_fusion
  11.3 1.7 fusion.2
  13.7 1.4 fusion.6
  15.1 1.8 fusion.5
  16.9 1.0 slice.43
  17.9 0.0 all-gather.5.cloned.1.call-update
  17.9 0.0 copy-start.8
  17.9 7.9 %all-to-all-start = ((bf16[8,64,1152]{2,1,0:T(8,128)(2,1)}), bf16[8,64,1152]{2,1,0:T(8,128)(2,1)}, u32[]{:S(2)}, u32[]{:S(2)}) async-start(bf16[8,64,1152]{2,1,0:T(8,128)(2,1)} %bitcast.1), calls=%async_computation | async-start | bytes 2359296 | tf_op jit(solution)/shard_map/all_to_all | solution.py:284
  25.8 0.0 all-gather.7.cloned.1.call-start
  25.9 0.8 slice.44.refs_0_
  26.6 0.6 dynamic_slice.34
  29.0 1.1 copy.25
  30.0 5.1 %constant_dynamic-slice_fusion.4 = (bf16[1,1,300,1152]{3,1,2,0:T(2,128)(2,1)}, bf16[1,1,300,1152]{3,1,2,0:T(2,128)(2,1)S(1)}) fusion(bf16[2,2,300,1152]{3,1,2,0:T(2,128)(2,1)} %param.21, s32[]{:T(128)S(6)} %select_n.36, s32[]{:T(128)S(6)} %add.86), kind=kLoop, calls=%fused_computation.22 | loop fusion | bytes 2764808 | tf_op jit(solution)/shard_map/slice | solution.py:292
  35.1 3.6 %copy.28 = bf16[1,1,300,1152]{2,3,1,0:T(8,128)(2,1)S(1)} copy(bf16[1,1,300,1152]{3,1,2,0:T(2,128)(2,1)} %get-tuple-element.25) | data formatting | bytes 1382400
  38.8 2.0 pad.14.refs_1_.refs_6_.refs_2_
  40.8 1.1 pad.13.refs_2_
  41.9 2.1 copy.27
  44.0 0.8 copy.24
  44.8 0.0 copy-start.4
  44.8 0.0 copy-start.5
  44.8 0.0 copy-start.6
  44.8 1.6 pad.12.refs_1_
  46.5 0.9 pad_maximum_fusion.refs_5_.refs_0_
  47.3 7.4 %all-to-all-done = bf16[8,64,1152]{2,1,0:T(8,128)(2,1)} async-done(((bf16[8,64,1152]{2,1,0:T(8,128)(2,1)}), bf16[8,64,1152]{2,1,0:T(8,128)(2,1)}, u32[]{:S(2)}, u32[]{:S(2)}) %all-to-all-start) | async-done | bytes 1179680 | tf_op jit(solution)/shard_map/all_to_all | solution.py:284
  54.8 1.6 slice_bitcast_fusion.refs_0_
  56.4 51.3 %all-gather.5.cloned.1.call-done.refs_0_.refs_1_ = bf16[6144,1152]{1,0:T(8,128)(2,1)} async-done(((bf16[384,1152]{1,0:T(8,128)(2,1)}), bf16[6144,1152]{1,0:T(8,128)(2,1)}) %all-gather.5.cloned.1.call-update) | async-done | bytes 14155792 | tf_op jit(solution)/shard_map/all_gather | solution.py:172
  107.7 0.0 all-gather.7.cloned.1.call-update
  107.7 0.2 all-gather.9.cloned.1.call-start
  107.9 10.5 %project.2 = (bf16[6144,128]{1,0:T(8,128)(2,1)}, bf16[128,6144]{1,0:T(8,128)(2,1)}, bf16[6144,128]{1,0:T(8,128)(2,1)}) custom-call(bf16[6144,1152]{1,0:T(8,128)(2,1)} %all-gather.5.cloned.1.call-done.refs_0_.refs_1_, bf16[1152,256]{1,0:T(8,128)(2,1)} %pad.14.refs_1_.refs_6_.refs_2_), custom_call_target="tpu_custom_call" | custom-call | flops 3623878656 | bytes 18874368 | tf_op jit(solution)/shard_map/project/pallas_call | solution.py:60
  118.4 0.0 all-gather.9.cloned.1.call-update
  118.5 50.7 %self_attend.3.refs_0_.refs_4_ = f32[6144,128]{1,0:T(8,128)} custom-call(bf16[6144,128]{1,0:T(8,128)(2,1)} %get-tuple-element.15.refs_0_.refs_1_, bf16[128,6144]{1,0:T(8,128)(2,1)} %get-tuple-element.16.refs_1_.refs_2_, bf16[6144,128]{1,0:T(8,128)(2,1)} %get-tuple-element.17.refs_2_.refs_4_), custom_call_target="tpu_custom_call" | custom-call | flops 38654705664 | bytes 4194304 | tf_op jit(solution)/shard_map/self_attend/pallas_call | solution.py:149
  169.1 4.5 %project.3 = (bf16[2048,128]{1,0:T(8,128)(2,1)}, bf16[128,2048]{1,0:T(8,128)(2,1)}, bf16[2048,128]{1,0:T(8,128)(2,1)}) custom-call(f32[6144,128]{1,0:T(8,128)} %self_attend.3.refs_0_.refs_4_, bf16[2048,1152]{1,0:T(8,128)(2,1)} %all-gather.7.cloned.1.call-done.refs_1_, bf16[1152,256]{1,0:T(8,128)(2,1)} %pad.14.refs_1_.refs_6_.refs_2_), custom_call_target="tpu_custom_call" | custom-call | flops 1207959552 | bytes 6291456 | tf_op jit(solution)/shard_map/project/pallas_call | solution.py:60
  173.7 20.9 %self_attend.4.refs_0_ = bf16[16,72,384]{2,1,0:T(8,128)(2,1)} custom-call(f32[6144,128]{1,0:T(8,128)} %self_attend.3.refs_0_.refs_4_, bf16[6144,128]{1,0:T(8,128)(2,1)} %get-tuple-element.15.refs_0_.refs_1_, bf16[128,2048]{1,0:T(8,128)(2,1)} %get-tuple-element.20.refs_2_.refs_3_, bf16[2048,128]{1,0:T(8,128)(2,1)} %get-tuple-element.21.refs_3_.refs_5_, ...), custom_call_target="tpu_custom_call" | custom-call | flops 12884901888 | bytes 4194304 | tf_op jit(solution)/shard_map/self_attend/pallas_call | solution.py:149
  194.5 5.6 %all-to-all-start.1 = ((bf16[16,72,384]{2,1,0:T(8,128)(2,1)}), bf16[16,72,384]{2,1,0:T(8,128)(2,1)S(1)}, u32[]{:S(2)}, u32[]{:S(2)}) async-start(bf16[16,72,384]{2,1,0:T(8,128)(2,1)} %self_attend.4.refs_0_), calls=%async_computation.1 | async-start | bytes 1769472 | tf_op jit(solution)/shard_map/all_to_all | solution.py:310
  200.1 24.2 %self_attend.5.refs_0_ = bf16[16,72,128]{2,1,0:T(8,128)(2,1)} custom-call(bf16[16,72,384]{2,1,0:T(8,128)(2,1)} %self_attend.4.refs_0_, bf16[2048,128]{1,0:T(8,128)(2,1)} %get-tuple-element.22.refs_1_, bf16[128,6144]{1,0:T(8,128)(2,1)} %get-tuple-element.16.refs_1_.refs_2_, bf16[128,2048]{1,0:T(8,128)(2,1)} %get-tuple-element.20.refs_2_.refs_3_, ...), custom_call_target="tpu_custom_call" | custom-call | flops 17179869184 | bytes 4194304 | tf_op jit(solution)/shard_map/self_attend/pallas_call | solution.py:149
  224.3 1.0 copy-done.3
  225.2 14.5 %all_to_all.25 = bf16[16,72,128]{2,1,0:T(8,128)(2,1)} all-to-all(bf16[16,72,128]{2,1,0:T(8,128)(2,1)} %link.6), channel_id=1, replica_groups=mesh['step'=8,'tok'=16] {'tok'}, dimensions={0} | all-to-all | bytes 589824 | tf_op jit(solution)/shard_map/all_to_all | solution.py:310
  239.7 16.3 %finish.1 = bf16[512,1152]{1,0:T(8,128)(2,1)} custom-call(bf16[1152,384]{1,0:T(8,128)(2,1)} %bitcast.38, bf16[1152,128]{1,0:T(8,128)(2,1)} %bitcast.41, bf16[512,1152]{1,0:T(8,128)(2,1)} %bitcast.8.refs_2_, f32[1,1152]{1,0:T(1,128)} %get-tuple-element.27.refs_3_, bf16[16,3,72,1152]{3,2,1,0:T(8,128)(2,1)} %bitcast.42, ...), custom_call_target="tpu_custom_call" | custom-call | flops 6794772480 | bytes 10485760 | tf_op jit(solution)/shard_map/finish/pallas_call | solution.py:226
  256.0 7.2 %all-to-all-start.3 = ((bf16[8,64,1152]{2,1,0:T(8,128)(2,1)}), bf16[8,64,1152]{2,1,0:T(8,128)(2,1)S(1)}, u32[]{:S(2)}, u32[]{:S(2)}) async-start(bf16[8,64,1152]{2,1,0:T(8,128)(2,1)} %bitcast.40), calls=%async_computation.3 | async-start | bytes 2359296 | tf_op jit(solution)/shard_map/all_to_all | solution.py:284
  263.2 0.1 compare_select_fusion
  263.3 0.6 gather_fusion
  263.9 0.7 and_select_fusion.coefs
  264.6 16.8 %all-to-all-done.3.everyone = bf16[8,64,1152]{2,1,0:T(8,128)(2,1)S(1)} async-done(((bf16[8,64,1152]{2,1,0:T(8,128)(2,1)}), bf16[8,64,1152]{2,1,0:T(8,128)(2,1)S(1)}, u32[]{:S(2)}, u32[]{:S(2)}) %all-to-all-start.3) | async-done | bytes 1179680 | tf_op jit(solution)/shard_map/all_to_all | solution.py:284
  281.3 1.0 copy-done.2
  282.4 3.4 %scan.1 = bf16[8,64,1152]{2,1,0:T(8,128)(2,1)} custom-call(f32[8]{0:T(128)} %and_select_fusion.coefs, bf16[64,1152]{1,0:T(8,128)(2,1)} %get-tuple-element.14.refs_2_.first, bf16[8,64,1152]{2,1,0:T(8,128)(2,1)} %copy-done.2), custom_call_target="tpu_custom_call" | custom-call | tf_op jit(solution)/shard_map/scan/pallas_call | solution.py:249
  285.7 21.5 %all_to_all.26 = bf16[8,64,1152]{2,1,0:T(8,128)(2,1)S(1)} all-to-all(bf16[8,64,1152]{2,1,0:T(8,128)(2,1)} %scan.1), channel_id=1, replica_groups=mesh['step'=8,'tok'=16] {'step'}, dimensions={0} | all-to-all | bytes 2359296 | tf_op jit(solution)/shard_map/all_to_all | solution.py:284
  307.2 1.0 copy.37
  (26 shorter events, 0.2 us)
Async XLA Ops:
  6.5 22.4 %copy-start = (bf16[2,1152,1,216]{1,3,2,0:T(8,128)(2,1)S(1)}, bf16[2,1152,1,216]{1,3,2,0:T(8,128)(2,1)}, u32[]{:S(2)}) copy-start(bf16[2,1152,1,216]{1,3,2,0:T(8,128)(2,1)} %param.17) | copy-start | bytes 2985988
  6.5 101.2 %all-gather.5.cloned.1.call-start = ((), (), s32[]{:S(2)}) async-start(), calls=%async_computation.5 | async-start | bytes 15040512 | tf_op jit(solution)/shard_map/all_gather | solution.py:172
  17.9 8.7 %copy-start.8 = (s32[32]{0:T(128)S(1)}, s32[32]{0:T(128)}, u32[]{:S(2)}) copy-start(s32[32]{0:T(128)} %param.13) | copy-start | bytes 388
  17.9 36.9 %all-to-all-start = ((bf16[8,64,1152]{2,1,0:T(8,128)(2,1)}), bf16[8,64,1152]{2,1,0:T(8,128)(2,1)}, u32[]{:S(2)}, u32[]{:S(2)}) async-start(bf16[8,64,1152]{2,1,0:T(8,128)(2,1)} %bitcast.1), calls=%async_computation | async-start | bytes 2359296 | tf_op jit(solution)/shard_map/all_to_all | solution.py:284
  25.8 143.3 %all-gather.7.cloned.1.call-start = ((), (), s32[]{:S(2)}) async-start(), calls=%async_computation.6 | async-start | bytes 5013504 | tf_op jit(solution)/shard_map/all_gather | solution.py:172
  44.8 1.6 copy-start.4
  44.8 1.6 copy-start.5
  44.8 1.6 copy-start.6
  107.7 132.0 %all-gather.9.cloned.1.call-start = ((), (), s32[]{:S(2)}) async-start(), calls=%async_computation.7 | async-start | bytes 8460288 | tf_op jit(solution)/shard_map/all_gather | solution.py:305
  194.5 29.7 %all-to-all-start.1 = ((bf16[16,72,384]{2,1,0:T(8,128)(2,1)}), bf16[16,72,384]{2,1,0:T(8,128)(2,1)S(1)}, u32[]{:S(2)}, u32[]{:S(2)}) async-start(bf16[16,72,384]{2,1,0:T(8,128)(2,1)} %self_attend.4.refs_0_), calls=%async_computation.1 | async-start | bytes 1769472 | tf_op jit(solution)/shard_map/all_to_all | solution.py:310
  224.2 1.0 copy-start.3
  256.0 7.2 %copy-start.7 = (s32[32]{0:T(128)S(1)}, s32[32]{0:T(128)}, u32[]{:S(2)}) copy-start(s32[32]{0:T(128)} %param.12) | copy-start | bytes 388
  256.0 7.3 %copy-start.1 = (f32[64]{0:T(128)S(1)}, f32[64]{0:T(128)}, u32[]{:S(2)}) copy-start(f32[64]{0:T(128)} %param.16) | copy-start | bytes 772
  256.0 25.3 %all-to-all-start.3 = ((bf16[8,64,1152]{2,1,0:T(8,128)(2,1)}), bf16[8,64,1152]{2,1,0:T(8,128)(2,1)S(1)}, u32[]{:S(2)}, u32[]{:S(2)}) async-start(bf16[8,64,1152]{2,1,0:T(8,128)(2,1)} %bitcast.40), calls=%async_computation.3 | async-start | bytes 2359296 | tf_op jit(solution)/shard_map/all_to_all | solution.py:284
  281.3 1.0 copy-start.2
Sparse Core Ops, SparseCore 0:
  18.0 89.6 all-gather.4
  109.4 40.6 all-gather.6
  151.8 50.1 all-gather.8

commit v3 on v2

--- a/solution.py
+++ b/solution.py
@@ -15,8 +15,10 @@
 CHUNKS = (384, 128)
 SOURCES = (2, 8)
 ROW_BLOCK = 1024
+ROWS = 128
 KEY_BLOCK = 1024
 HALVES = 2
+STRIP = 32
 VALUE = 2 * HEAD - LANES
 FACTOR = math.log2(math.e) / HEAD**0.5
 VMEM_LIMIT = 60 * 2**20
@@ -39,6 +41,50 @@
 
 def whole(array):
     return pl.BlockSpec(array.shape, lambda *_: (0,) * len(array.shape))
+
+
+def norm_kernel(entry, latent, modulation, *outs):
+    flat = latent[...].astype(jnp.float32)
+    mean = jnp.mean(flat, axis=1, keepdims=True)
+    centred = flat - mean
+    var = jnp.mean(centred**2, axis=1, keepdims=True)
+    row = pl.ds(entry[0] % 8, 1)
+    shift, scale = modulation[0, row, :], modulation[1, row, :]
+    normed = (centred * lax.rsqrt(var + 1e-06) * (1.0 + scale) + shift).astype(jnp.bfloat16)
+    here = pl.program_id(0)
+    first = CHUNKS[0] // ROWS
+
+    @pl.when(here < first)
+    def _():
+        outs[0][...] = normed
+
+    @pl.when(here >= first)
+    def _():
+        outs[1][...] = normed
+
+
+def norm(latent, modulation, entry):
+    count, width = latent.shape
+    first = CHUNKS[0] // ROWS
+    block = (ROWS, width)
+    return pl.pallas_call(
+        norm_kernel,
+        grid_spec=pltpu.PrefetchScalarGridSpec(
+            num_scalar_prefetch=1,
+            grid=(count // ROWS,),
+            in_specs=[
+                pl.BlockSpec(block, lambda i, entry: (i, 0)),
+                pl.BlockSpec((3, 8, width), lambda i, entry: (0, entry[0] // 8, 0)),
+            ],
+            out_specs=[
+                pl.BlockSpec(block, lambda i, entry: (jnp.minimum(i, first - 1), 0)),
+                pl.BlockSpec(block, lambda i, entry: (jnp.maximum(i - first, 0), 0)),
+            ],
+        ),
+        out_shape=[jax.ShapeDtypeStruct((per, width), jnp.bfloat16) for per in CHUNKS],
+        compiler_params=pltpu.CompilerParams(vmem_limit_bytes=VMEM_LIMIT),
+        name="norm",
+    )(entry, latent, modulation)
 
 
 def project_kernel(waited, *refs):
@@ -81,7 +127,7 @@
     values = refs[key_chunks : 2 * key_chunks]
     del refs[: 2 * key_chunks]
     state = refs.pop(0) if carried else None
-    out, scores = refs
+    out, scores, exps = refs
     parts = [
         (key, value, slice(start, start + KEY_BLOCK))
         for key, value in zip(keys, values)
@@ -98,21 +144,30 @@
             query_ref[spans[half], :], key[:, span], preferred_element_type=jnp.float32
         )
 
+    strips = [slice(start, start + STRIP) for start in range(0, rows, STRIP)]
     totals = [state[span, :] if carried else None for span in spans]
-    tops = [total[:, LANES - 1 :] if carried else None for total in totals]
+    tops = [
+        [total[strip, LANES - 1 :] if carried else None for strip in strips] for total in totals
+    ]
     scores[0] = score(units[0])
     for index, (half, step) in enumerate(units):
         if index + 1 < len(units):
             scores[(index + 1) % 2] = score(units[index + 1])
-        now = scores[index % 2]
-        top, total = tops[half], totals[half]
-        high = jnp.max(now, axis=1, keepdims=True)
-        newer = high if top is None else jnp.maximum(top, high)
-        weights = jnp.exp2(now * FACTOR - newer * FACTOR).astype(jnp.bfloat16)
+        fresh = tops[half][0] is None
+        shrink = []
+        for place, strip in enumerate(strips):
+            now = scores[index % 2, strip, :]
+            top = tops[half][place]
+            high = jnp.max(now, axis=1, keepdims=True)
+            newer = high if fresh else jnp.maximum(top, high)
+            exps[strip, :] = jnp.exp2(now * FACTOR - newer * FACTOR).astype(jnp.bfloat16)
+            if not fresh:
+                shrink.append(jnp.exp2((top - newer) * FACTOR))
+            tops[half][place] = newer
         _, value, span = parts[step]
-        part = jnp.dot(weights, value[span, :], preferred_element_type=jnp.float32)
-        totals[half] = part if top is None else total * jnp.exp2((top - newer) * FACTOR) + part
-        tops[half] = newer
+        part = jnp.dot(exps[...], value[span, :], preferred_element_type=jnp.float32)
+        totals[half] = part if fresh else totals[half] * jnp.concatenate(shrink, 0) + part
+    tops = [jnp.concatenate(top, 0) for top in tops]
     for half, (total, top) in enumerate(zip(totals, tops)):
         if final:
             turned = total.T
@@ -151,7 +206,10 @@
         grid=(count // block,),
         in_specs=in_specs,
         out_specs=out_spec,
-        scratch_shapes=[pltpu.VMEM((2, block // HALVES, KEY_BLOCK), jnp.float32)],
+        scratch_shapes=[
+            pltpu.VMEM((2, block // HALVES, KEY_BLOCK), jnp.float32),
+            pltpu.VMEM((block // HALVES, KEY_BLOCK), jnp.bfloat16),
+        ],
         out_shape=out_shape,
         compiler_params=pltpu.CompilerParams(vmem_limit_bytes=VMEM_LIMIT),
         cost_estimate=pl.CostEstimate(
@@ -162,16 +220,15 @@
 
 
 def self_attend(normed, weights, early):
-    chunks, states, previous, start = [], [], [], 0
+    chunks, states, previous = [], [], []
     held = None
-    for chunk, per in enumerate(CHUNKS):
-        own = normed[start : start + per]
-        start += per
+    for chunk in range(len(CHUNKS)):
+        own = normed[chunk]
         if held is not None:
             own = link([own], [held] + early[chunk])[0]
         held = lax.all_gather(own, "tok", axis=0, tiled=True)
         chunks.append([held])
-    for chunk, per in enumerate(CHUNKS):
+    for chunk in range(len(CHUNKS)):
         last = chunk + 1 == len(CHUNKS)
         chunks[chunk] = project(chunks[chunk][0], weights, previous)
         for earlier in range(chunk + 1):
@@ -186,11 +243,19 @@
 
 
 def finish_kernel(parts, *refs):
-    turned, (latent, gate, weights, keys, values, out, cross) = refs[:parts], refs[parts:]
+    turned, (latent, gate, weights, keys, values) = refs[:parts], refs[parts : parts + 5]
+    out, cross, near, arrived = refs[parts + 5 :]
     width = latent.shape[1]
+    copies = [
+        pltpu.make_async_copy(weights.at[:, index], near.at[index], arrived.at[index])
+        for index in range(3)
+    ]
+    for copy in copies:
+        copy.start()
 
     def weight(index):
-        return weights[:, index].astype(jnp.float32).reshape(width, width).astype(jnp.bfloat16)
+        copies[index].wait()
+        return near[index].astype(jnp.float32).reshape(width, width).astype(jnp.bfloat16)
 
     attended = jnp.concatenate([part[...].astype(jnp.float32) for part in turned], 1)
     attended = attended.T.astype(jnp.bfloat16)
@@ -222,14 +287,21 @@
 
 def finish(turned, latent, gate, weights, keys, values):
     count, width = latent.shape
+    heads = width // HEAD
     args = (*turned, latent, gate, weights, keys, values)
     return pl.pallas_call(
         functools.partial(finish_kernel, len(turned)),
         grid=(1,),
-        in_specs=[whole(arg) for arg in args],
+        in_specs=[
+            pl.BlockSpec(memory_space=pl.ANY) if arg is weights else whole(arg) for arg in args
+        ],
         out_specs=whole(latent),
         out_shape=jax.ShapeDtypeStruct((count, width), jnp.bfloat16),
-        scratch_shapes=[pltpu.VMEM((width, count), jnp.float32)],
+        scratch_shapes=[
+            pltpu.VMEM((width, count), jnp.float32),
+            pltpu.VMEM((3, heads, HEAD, width), jnp.bfloat16),
+            pltpu.SemaphoreType.DMA((3,)),
+        ],
         compiler_params=pltpu.CompilerParams(vmem_limit_bytes=VMEM_LIMIT),
         cost_estimate=pl.CostEstimate(
             flops=10 * count * width * width, bytes_accessed=10 * 2**20, transcendentals=0
@@ -250,12 +322,12 @@
         scan_kernel,
         grid_spec=pltpu.PrefetchScalarGridSpec(
             num_scalar_prefetch=1,
-            grid=(1,),
-            in_specs=[whole(first), whole(everyone)],
-            out_specs=whole(everyone),
+            grid=(),
+            in_specs=[pl.BlockSpec(memory_space=pltpu.VMEM)] * 2,
+            out_specs=pl.BlockSpec(memory_space=pltpu.VMEM),
         ),
         out_shape=jax.ShapeDtypeStruct(everyone.shape, jnp.bfloat16),
-        compiler_params=pltpu.CompilerParams(vmem_limit_bytes=VMEM_LIMIT),
+        compiler_params=pltpu.CompilerParams(vmem_limit_bytes=16 * 2**20),
         name="scan",
     )(coefs, first, everyone)
 
@@ -270,12 +342,7 @@
     latent = latents[0]
     count, width = latent.shape
     heads = width // HEAD
-    flat = latent.astype(jnp.float32)
-    mean = jnp.mean(flat, axis=1, keepdims=True)
-    var = jnp.mean((flat - mean) ** 2, axis=1, keepdims=True)
-    normed = ((flat - mean) * lax.rsqrt(var + 1e-06) * (1.0 + modulate[1]) + modulate[0]).astype(
-        jnp.bfloat16
-    )
+    normed = norm(latent, jnp.swapaxes(modulation, 0, 1), entry[None])
     own_qkv = lax.dynamic_index_in_dim(w_qkv, expert, 0, False)[:, 0, :]
     w_mixed = jnp.pad(own_qkv, ((0, 0), (0, 2 * LANES - 3 * HEAD)))
 
@@ -311,7 +378,7 @@
         return back.reshape(width, -1)
 
     turned = [returned(heads_out[0])]
-    turned.append(returned(link([heads_out[1]], turned)[0]))
+    turned.append(returned(link([heads_out[1]], [turned[0], all_weights])[0]))
     predicted = finish(turned, latent, modulate[2][None], all_weights, text_keys, text_values)
     coefs = jnp.take(coef, lax.dynamic_slice_in_dim(timesteps, offset[0], steps))
     return over_steps(scan(coefs, first, over_steps(predicted))).reshape(1, count, width)

time: 321 us -> 317 us (0.988)
  blocking collectives: 36 us -> 21.3 us
  Pallas kernels: 130 us -> 137 us
  other arithmetic: 8.01 us -> 1.04 us
  starting transfers between devices: 20.9 us -> 26.9 us
  waiting for transfers between devices: 75.6 us -> 81.5 us
    all_to_all x1 -> x0, blocking collectives: 14.5 us -> none  [returned(): back = lax.all_to_all(value, 'tok', split_axis=0, concat_axis=0, tiled=True)]
    all_to_all x1 -> x2, starting transfers between devices: 5.55 us -> 11.5 us  [returned(): back = lax.all_to_all(value, 'tok', split_axis=0, concat_axis=0, tiled=True)]
    all_to_all x1 -> x2, waiting for transfers between devices: 0.01 us -> 4.99 us  [returned(): back = lax.all_to_all(value, 'tok', split_axis=0, concat_axis=0, tiled=True)]
    pallas_call x0 -> x1, Pallas kernels: none -> 4.84 us  [norm(): pl.pallas_call(norm_kernel, grid_spec=pltpu.PrefetchScalarGridSpec(num_sc...]
    pallas_call x3, Pallas kernels: 95.7 us -> 99 us  [attend_chunk(): pl.pallas_call(functools.partial(attend_kernel, len(after), len(sources),...]
    reduce_sum x2 -> x0, other arithmetic: 3.22 us -> none  [the longest x1 1.72 us: body(): var = jnp.mean((flat - mean) ** 2, axis=1, keepdims=True)]
    unnamed x21 -> x23, local copies, waits for them, and re-layouts: 8.74 us -> 8.45 us
  transfers between devices with their start and end apart: 6 -> 7, of which waited for: 3 -> 4; matrix products, arithmetic and copies ran while one was open for 7% -> 7% of each run, Pallas kernels for 35% -> 37%
where the time goes in v3:
time: 317 us; the launch traced here: 311 us
  Pallas kernels  137 us (43%)
  waiting for transfers between devices  81.5 us (26%)
  starting transfers between devices  26.9 us (8%)
  local copies, waits for them, and re-layouts  25.9 us (8%)
  blocking collectives  21.3 us (7%)
  between operations  18.4 us (6%)
    pallas_call x3, Pallas kernels, attend_chunk(): pl.pallas_call(functools.partial(attend_kernel, len(after), len(sources),...  99 us
    all_gather x2, waiting for transfers between devices, self_attend(): held = lax.all_gather(own, 'tok', axis=0, tiled=True)  51.3 us
    all_to_all x2, waiting for transfers between devices, over_steps(): lax.all_to_all(shaped, 'step', split_axis=0, concat_axis=0, tiled=True)  25.2 us
    all_to_all x1, blocking collectives, over_steps(): lax.all_to_all(shaped, 'step', split_axis=0, concat_axis=0, tiled=True)  21.3 us
    pallas_call x1, Pallas kernels, finish(): pl.pallas_call(functools.partial(finish_kernel, len(turned)), grid=(1,),...  16.7 us
    all_to_all x2, starting transfers between devices, over_steps(): lax.all_to_all(shaped, 'step', split_axis=0, concat_axis=0, tiled=True)  15.1 us
    pallas_call x2, Pallas kernels, project(): pl.pallas_call(functools.partial(project_kernel, len(after)), grid=(count...  15.1 us
    all_to_all x2, starting transfers between devices, returned(): back = lax.all_to_all(value, 'tok', split_axis=0, concat_axis=0, tiled=True)  11.5 us
  transfers between devices with their start and end apart: 7, of which 4 were waited for; matrix products, arithmetic and copies ran while one was open for 7% of the time, Pallas kernels for 37%

profile of v3, /device:TPU:0, one launch (start us, length us, event | category | flops | bytes accessed | tf_op | source)
XLA Modules:
  0.0 311.5 jit_solution(2418076233453260957)
XLA Ops:
  7.3 1.3 dynamic_slice.36.entry
  8.6 4.8 %norm.1 = (bf16[384,1152]{1,0:T(8,128)(2,1)}, bf16[128,1152]{1,0:T(8,128)(2,1)}) custom-call(s32[1]{0:T(128)} %dynamic_slice.36.entry, bf16[512,1152]{1,0:T(8,128)(2,1)} %bitcast.8.latent.refs_2_, f32[3,64,1152]{2,1,0:T(8,128)} %bitcast.41), custom_call_target="tpu_custom_call" | custom-call | tf_op jit(solution)/shard_map/norm/pallas_call | solution.py:70
  13.4 0.0 all-gather.5.cloned.1.call-update
  13.5 0.0 copy-start.9
  13.5 7.9 %all-to-all-start = ((bf16[8,64,1152]{2,1,0:T(8,128)(2,1)}), bf16[8,64,1152]{2,1,0:T(8,128)(2,1)}, u32[]{:S(2)}, u32[]{:S(2)}) async-start(bf16[8,64,1152]{2,1,0:T(8,128)(2,1)} %bitcast.1), calls=%async_computation | async-start | bytes 2359296 | tf_op jit(solution)/shard_map/all_to_all | solution.py:351
  21.4 0.0 all-gather.7.cloned.1.call-start
  21.4 0.6 dynamic_slice.34
  24.0 1.1 copy.25
  25.1 5.2 %constant_dynamic-slice_fusion.4 = (bf16[1,1,300,1152]{3,1,2,0:T(2,128)(2,1)}, bf16[1,1,300,1152]{3,1,2,0:T(2,128)(2,1)S(1)}) fusion(bf16[2,2,300,1152]{3,1,2,0:T(2,128)(2,1)} %param.21, s32[]{:T(128)S(6)} %select_n.36, s32[]{:T(128)S(6)} %add.42), kind=kLoop, calls=%fused_computation.12 | loop fusion | bytes 2764808 | tf_op jit(solution)/shard_map/slice | solution.py:359
  30.3 3.6 %copy.28 = bf16[1,1,300,1152]{2,3,1,0:T(8,128)(2,1)S(1)} copy(bf16[1,1,300,1152]{3,1,2,0:T(2,128)(2,1)} %get-tuple-element.27) | data formatting | bytes 1382400
  34.0 2.0 pad.14.refs_1_.refs_6_.refs_2_
  36.0 1.1 pad.13.refs_2_
  37.1 2.1 copy.27
  39.1 0.8 copy.24
  39.9 0.0 copy-start.5
  39.9 0.0 copy-start.6
  40.0 0.0 copy-start.7
  40.0 1.6 pad.12.refs_1_
  41.7 0.9 pad_maximum_fusion.refs_5_.refs_0_
  42.5 7.8 %all-to-all-done = bf16[8,64,1152]{2,1,0:T(8,128)(2,1)} async-done(((bf16[8,64,1152]{2,1,0:T(8,128)(2,1)}), bf16[8,64,1152]{2,1,0:T(8,128)(2,1)}, u32[]{:S(2)}, u32[]{:S(2)}) %all-to-all-start) | async-done | bytes 1179680 | tf_op jit(solution)/shard_map/all_to_all | solution.py:351
  50.4 1.6 slice_bitcast_fusion.refs_0_
  51.9 51.3 %all-gather.5.cloned.1.call-done.refs_0_.refs_1_ = bf16[6144,1152]{1,0:T(8,128)(2,1)} async-done(((bf16[384,1152]{1,0:T(8,128)(2,1)}), bf16[6144,1152]{1,0:T(8,128)(2,1)}) %all-gather.5.cloned.1.call-update) | async-done | bytes 14155792 | tf_op jit(solution)/shard_map/all_gather | solution.py:229
  103.2 0.0 all-gather.7.cloned.1.call-update
  103.3 0.2 all-gather.9.cloned.1.call-start
  103.5 10.5 %project.2 = (bf16[6144,128]{1,0:T(8,128)(2,1)}, bf16[128,6144]{1,0:T(8,128)(2,1)}, bf16[6144,128]{1,0:T(8,128)(2,1)}) custom-call(bf16[6144,1152]{1,0:T(8,128)(2,1)} %all-gather.5.cloned.1.call-done.refs_0_.refs_1_, bf16[1152,256]{1,0:T(8,128)(2,1)} %pad.14.refs_1_.refs_6_.refs_2_), custom_call_target="tpu_custom_call" | custom-call | flops 3623878656 | bytes 18874368 | tf_op jit(solution)/shard_map/project/pallas_call | solution.py:106
  114.0 0.0 all-gather.9.cloned.1.call-update
  114.0 52.3 %self_attend.3.refs_0_.refs_4_ = f32[6144,128]{1,0:T(8,128)} custom-call(bf16[6144,128]{1,0:T(8,128)(2,1)} %get-tuple-element.18.refs_0_.refs_1_, bf16[128,6144]{1,0:T(8,128)(2,1)} %get-tuple-element.19.refs_1_.refs_2_, bf16[6144,128]{1,0:T(8,128)(2,1)} %get-tuple-element.20.refs_2_.refs_4_), custom_call_target="tpu_custom_call" | custom-call | flops 38654705664 | bytes 4194304 | tf_op jit(solution)/shard_map/self_attend/pallas_call | solution.py:204
  166.4 4.6 %project.3 = (bf16[2048,128]{1,0:T(8,128)(2,1)}, bf16[128,2048]{1,0:T(8,128)(2,1)}, bf16[2048,128]{1,0:T(8,128)(2,1)}) custom-call(f32[6144,128]{1,0:T(8,128)} %self_attend.3.refs_0_.refs_4_, bf16[2048,1152]{1,0:T(8,128)(2,1)} %all-gather.7.cloned.1.call-done.refs_1_, bf16[1152,256]{1,0:T(8,128)(2,1)} %pad.14.refs_1_.refs_6_.refs_2_), custom_call_target="tpu_custom_call" | custom-call | flops 1207959552 | bytes 6291456 | tf_op jit(solution)/shard_map/project/pallas_call | solution.py:106
  171.0 21.9 %self_attend.4.refs_0_ = bf16[16,72,384]{2,1,0:T(8,128)(2,1)} custom-call(f32[6144,128]{1,0:T(8,128)} %self_attend.3.refs_0_.refs_4_, bf16[6144,128]{1,0:T(8,128)(2,1)} %get-tuple-element.18.refs_0_.refs_1_, bf16[128,2048]{1,0:T(8,128)(2,1)} %get-tuple-element.24.refs_2_.refs_3_, bf16[2048,128]{1,0:T(8,128)(2,1)} %get-tuple-element.25.refs_3_.refs_5_, ...), custom_call_target="tpu_custom_call" | custom-call | flops 12884901888 | bytes 4194304 | tf_op jit(solution)/shard_map/self_attend/pallas_call | solution.py:204
  192.8 5.4 %all-to-all-start.1 = ((bf16[16,72,384]{2,1,0:T(8,128)(2,1)}), bf16[16,72,384]{2,1,0:T(8,128)(2,1)S(1)}, u32[]{:S(2)}, u32[]{:S(2)}) async-start(bf16[16,72,384]{2,1,0:T(8,128)(2,1)} %self_attend.4.refs_0_), calls=%async_computation.1 | async-start | bytes 1769472 | tf_op jit(solution)/shard_map/all_to_all | solution.py:377
  198.2 24.8 %self_attend.5.refs_0_ = bf16[16,72,128]{2,1,0:T(8,128)(2,1)} custom-call(bf16[16,72,384]{2,1,0:T(8,128)(2,1)} %self_attend.4.refs_0_, bf16[2048,128]{1,0:T(8,128)(2,1)} %get-tuple-element.26.refs_1_, bf16[128,6144]{1,0:T(8,128)(2,1)} %get-tuple-element.19.refs_1_.refs_2_, bf16[128,2048]{1,0:T(8,128)(2,1)} %get-tuple-element.24.refs_2_.refs_3_, ...), custom_call_target="tpu_custom_call" | custom-call | flops 17179869184 | bytes 4194304 | tf_op jit(solution)/shard_map/self_attend/pallas_call | solution.py:204
  223.0 0.0 all-gather.9.cloned.1.call-done
  223.1 0.9 copy-done.3
  224.0 6.1 %all-to-all-start.2 = ((bf16[16,72,128]{2,1,0:T(8,128)(2,1)}), bf16[16,72,128]{2,1,0:T(8,128)(2,1)S(1)}, u32[]{:S(2)}, u32[]{:S(2)}) async-start(bf16[16,72,128]{2,1,0:T(8,128)(2,1)} %link.7), calls=%async_computation.2 | async-start | bytes 589824 | tf_op jit(solution)/shard_map/all_to_all | solution.py:377
  232.1 1.4 dynamic-slice_bitcast_fusion.1.refs_3_
  233.5 5.0 %all-to-all-done.2 = bf16[16,72,128]{2,1,0:T(8,128)(2,1)S(1)} async-done(((bf16[16,72,128]{2,1,0:T(8,128)(2,1)}), bf16[16,72,128]{2,1,0:T(8,128)(2,1)S(1)}, u32[]{:S(2)}, u32[]{:S(2)}) %all-to-all-start.2) | async-done | bytes 294944 | tf_op jit(solution)/shard_map/all_to_all | solution.py:377
  238.5 0.7 copy-done.4
  239.2 16.7 %finish.1 = bf16[512,1152]{1,0:T(8,128)(2,1)} custom-call(bf16[1152,384]{1,0:T(8,128)(2,1)} %bitcast.36, bf16[1152,128]{1,0:T(8,128)(2,1)} %bitcast.42, bf16[512,1152]{1,0:T(8,128)(2,1)} %bitcast.8.latent.refs_2_, f32[1,1152]{1,0:T(1,128)} %dynamic-slice_bitcast_fusion.1.refs_3_, bf16[16,3,72,1152]{3,2,1,0:T(8,128)(2,1)} %bitcast.32, ...), custom_call_target="tpu_custom_call" | custom-call | flops 6794772480 | bytes 10485760 | tf_op jit(solution)/shard_map/finish/pallas_call | solution.py:292
  255.9 0.0 copy-start.8
  255.9 0.0 copy-start.2
  256.0 7.2 %all-to-all-start.3 = ((bf16[8,64,1152]{2,1,0:T(8,128)(2,1)}), bf16[8,64,1152]{2,1,0:T(8,128)(2,1)S(1)}, u32[]{:S(2)}, u32[]{:S(2)}) async-start(bf16[8,64,1152]{2,1,0:T(8,128)(2,1)} %bitcast.40), calls=%async_computation.3 | async-start | bytes 2359296 | tf_op jit(solution)/shard_map/all_to_all | solution.py:351
  263.2 0.1 compare_select_fusion
  263.3 0.6 gather_fusion
  264.0 0.1 and_select_fusion.coefs
  264.0 17.4 %all-to-all-done.3.everyone = bf16[8,64,1152]{2,1,0:T(8,128)(2,1)S(1)} async-done(((bf16[8,64,1152]{2,1,0:T(8,128)(2,1)}), bf16[8,64,1152]{2,1,0:T(8,128)(2,1)S(1)}, u32[]{:S(2)}, u32[]{:S(2)}) %all-to-all-start.3) | async-done | bytes 1179680 | tf_op jit(solution)/shard_map/all_to_all | solution.py:351
  281.4 0.8 scan.1
  282.2 21.3 %all_to_all.25 = bf16[8,64,1152]{2,1,0:T(8,128)(2,1)S(1)} all-to-all(bf16[8,64,1152]{2,1,0:T(8,128)(2,1)S(1)} %scan.1), channel_id=1, replica_groups=mesh['step'=8,'tok'=16] {'step'}, dimensions={0} | all-to-all | bytes 2359296 | tf_op jit(solution)/shard_map/all_to_all | solution.py:351
  303.5 1.0 copy.37
  (23 shorter events, 0.1 us)
Async XLA Ops:
  6.5 17.4 %copy-start = (bf16[2,1152,1,216]{1,3,2,0:T(8,128)(2,1)S(1)}, bf16[2,1152,1,216]{1,3,2,0:T(8,128)(2,1)}, u32[]{:S(2)}) copy-start(bf16[2,1152,1,216]{1,3,2,0:T(8,128)(2,1)} %param.17) | copy-start | bytes 2985988
  6.5 96.7 %all-gather.5.cloned.1.call-start = ((), (), s32[]{:S(2)}) async-start(), calls=%async_computation.5 | async-start | bytes 15040512 | tf_op jit(solution)/shard_map/all_gather | solution.py:229
  13.5 7.9 %copy-start.9 = (s32[32]{0:T(128)S(1)}, s32[32]{0:T(128)}, u32[]{:S(2)}) copy-start(s32[32]{0:T(128)} %param.13) | copy-start | bytes 388
  13.5 36.9 %all-to-all-start = ((bf16[8,64,1152]{2,1,0:T(8,128)(2,1)}), bf16[8,64,1152]{2,1,0:T(8,128)(2,1)}, u32[]{:S(2)}, u32[]{:S(2)}) async-start(bf16[8,64,1152]{2,1,0:T(8,128)(2,1)} %bitcast.1), calls=%async_computation | async-start | bytes 2359296 | tf_op jit(solution)/shard_map/all_to_all | solution.py:351
  21.4 145.0 %all-gather.7.cloned.1.call-start = ((), (), s32[]{:S(2)}) async-start(), calls=%async_computation.6 | async-start | bytes 5013504 | tf_op jit(solution)/shard_map/all_gather | solution.py:229
  39.9 1.6 copy-start.5
  39.9 1.6 copy-start.6
  40.0 1.6 copy-start.7
  103.3 119.8 %all-gather.9.cloned.1.call-start = ((), (), s32[]{:S(2)}) async-start(), calls=%async_computation.7 | async-start | bytes 8460288 | tf_op jit(solution)/shard_map/all_gather | solution.py:372
  192.8 30.2 %all-to-all-start.1 = ((bf16[16,72,384]{2,1,0:T(8,128)(2,1)}), bf16[16,72,384]{2,1,0:T(8,128)(2,1)S(1)}, u32[]{:S(2)}, u32[]{:S(2)}) async-start(bf16[16,72,384]{2,1,0:T(8,128)(2,1)} %self_attend.4.refs_0_), calls=%async_computation.1 | async-start | bytes 1769472 | tf_op jit(solution)/shard_map/all_to_all | solution.py:377
  223.0 1.0 copy-start.3
  224.0 14.5 %all-to-all-start.2 = ((bf16[16,72,128]{2,1,0:T(8,128)(2,1)}), bf16[16,72,128]{2,1,0:T(8,128)(2,1)S(1)}, u32[]{:S(2)}, u32[]{:S(2)}) async-start(bf16[16,72,128]{2,1,0:T(8,128)(2,1)} %link.7), calls=%async_computation.2 | async-start | bytes 589824 | tf_op jit(solution)/shard_map/all_to_all | solution.py:377
  238.5 0.7 copy-start.4
  255.9 7.3 %copy-start.8 = (s32[32]{0:T(128)S(1)}, s32[32]{0:T(128)}, u32[]{:S(2)}) copy-start(s32[32]{0:T(128)} %param.12) | copy-start | bytes 388
  255.9 7.4 %copy-start.2 = (f32[64]{0:T(128)S(1)}, f32[64]{0:T(128)}, u32[]{:S(2)}) copy-start(f32[64]{0:T(128)} %param.16) | copy-start | bytes 772
  256.0 25.4 %copy-start.1 = (bf16[64,1152]{1,0:T(8,128)(2,1)S(1)}, bf16[64,1152]{1,0:T(8,128)(2,1)}, u32[]{:S(2)}) copy-start(bf16[64,1152]{1,0:T(8,128)(2,1)} %get-tuple-element.16.refs_2_.first) | copy-start | bytes 442372
  256.0 25.4 %all-to-all-start.3 = ((bf16[8,64,1152]{2,1,0:T(8,128)(2,1)}), bf16[8,64,1152]{2,1,0:T(8,128)(2,1)S(1)}, u32[]{:S(2)}, u32[]{:S(2)}) async-start(bf16[8,64,1152]{2,1,0:T(8,128)(2,1)} %bitcast.40), calls=%async_computation.3 | async-start | bytes 2359296 | tf_op jit(solution)/shard_map/all_to_all | solution.py:351
Sparse Core Ops, SparseCore 0:
  13.6 89.6 all-gather.4
  104.9 40.6 all-gather.6
  147.4 50.1 all-gather.8
